TPU v7x, 256 devices: a whole 4x4x8 slice. The times are simulated.
256 devices in a mesh: batch: 16 (over z, core), vocab: 16 (over x, y).
Axes of the slice: x: 4, y: 4, z: 8, core: 2. Of those that a mesh axis runs over, the one named last changes fastest.
Arguments:
- queries: bfloat16 [256, 8192], P('batch'), may hold values from -6 to 8
- key_new: bfloat16 [256, 1024], P('batch'), may hold values from -6 to 6
- value_new: bfloat16 [256, 1024], P('batch'), may hold values from -6 to 6
- key_cache: bfloat16 [256, 256, 1024], P('batch', 'vocab'), may hold values from -6 to 6
- value_cache: bfloat16 [256, 256, 1024], P('batch', 'vocab'), may hold values from -6 to 6
- parents: int32 [256], replicated, may hold values from 0 to 255, as said below
- tokens: int32 [256], replicated, may hold values from 0 to 128255
- hidden: bfloat16 [256, 8192], P(None, 'batch'), may hold values from -40 to 40
- out_weight: bfloat16 [8192, 8192], P('vocab', 'batch'), may hold values from -4.5 to 4.5
- final_gain: float32 [8192], P('batch'), may hold values from 0.5 to 1.5
- head_weight: bfloat16 [128256, 8192], P(('batch', 'vocab')), may hold values from -3.25 to 3.25
- past_scores: float32 [256, 128256], P(None, ('batch', 'vocab')), may hold values from -3 to -0.5
Outputs:
- next_keys: bfloat16 [256, 256, 1024], P('batch', 'vocab')
- next_values: bfloat16 [256, 256, 1024], P('batch', 'vocab')
- candidates: float32 [256, 128256], P(None, ('batch', 'vocab'))
Inputs may be any that keep to these rules, and one draw needn't show every extreme that they name: Hypothesis i, in block b = i // 16 at row r = i % 16, is beam b // 2 of request ((b % 2 - b // 2) mod 2) * 16 + r, and parents[i] is a hypothesis of the same request. Within each aligned block of 16 hypotheses, at most 4 have their parents in any one aligned block of 16 hypotheses, and every block reaches 4.
All inputs are finite; a program needn't handle non-finite values.
Results may differ from a plain program's by a relative error of at most 0.0052.
Values may be sent and summed in bfloat16 or wider, within the bound.
A program may use at most 128 MiB of HBM per device.

v0:
```python
import jax
import jax.numpy as jnp
from jax import lax
from jax.sharding import PartitionSpec as P

D = 8192
HEADS = 64
KV_HEADS = 8
HEAD_DIM = 128


def joined(part, axis, combine):
    gathered = jax.tree.map(lambda a: lax.all_gather(a, axis), part)

    def take(source):
        return jax.tree.map(lambda a: lax.dynamic_index_in_dim(a, source, 0, False), gathered)

    return lax.fori_loop(
        1, lax.axis_size(axis), lambda source, state: combine(state, take(source)), take(0)
    )


def routing(parents, batch_count, rows_dev):
    parent_table = parents.reshape(batch_count, rows_dev)
    source = parent_table // rows_dev
    source_row = parent_table % rows_dev
    earlier_row = jnp.arange(rows_dev)[:, None] > jnp.arange(rows_dev)[None, :]
    same_source = source[:, :, None] == source[:, None, :]
    slot_index = jnp.sum(jnp.logical_and(same_source, earlier_row[None, :, :]), axis=2)
    return (source, source_row, slot_index)


def combine_pairs(earlier, latter):
    highest = jnp.maximum(earlier[0], latter[0])
    return (
        highest,
        earlier[1] * jnp.exp(earlier[0] - highest) + latter[1] * jnp.exp(latter[0] - highest),
    )


def attend(query_rows, key_rows, value_rows):
    row_count, positions, kv_cols = key_rows.shape
    group_size = HEADS // KV_HEADS
    query_groups = query_rows.reshape(row_count, KV_HEADS, HEAD_DIM, group_size)
    key_groups = key_rows.reshape(row_count, positions, KV_HEADS, HEAD_DIM)
    scores = jnp.einsum(
        "ngde,npgd->ngep", query_groups, key_groups, preferred_element_type=jnp.float32
    ) * HEAD_DIM ** (-0.5)
    local_max = jnp.max(scores, axis=3)
    local_sum = jnp.sum(jnp.exp(scores - local_max[..., None]), axis=3)
    largest, total = joined((local_max, local_sum), "vocab", combine_pairs)
    rounded = (jnp.exp(scores - largest[..., None]) / total[..., None]).astype(jnp.bfloat16)
    value_groups = value_rows.reshape(row_count, positions, KV_HEADS, HEAD_DIM)
    mixture = jnp.einsum(
        "ngep,npgd->ngde", rounded, value_groups, preferred_element_type=jnp.float32
    )
    summed = lax.psum_scatter(
        mixture.reshape(row_count, -1), "vocab", scatter_dimension=1, tiled=True
    )
    return summed.astype(jnp.bfloat16)


def body(
    queries,
    key_new,
    value_new,
    key_cache,
    value_cache,
    parents,
    tokens,
    hidden,
    out_weight,
    final_gain,
    head_weight,
    past_scores,
):
    batch_count = lax.axis_size("batch")
    my_index = lax.axis_index("batch")
    rows_dev, positions, kv_cols = key_cache.shape
    capacity = rows_dev // 4
    holds_last = lax.axis_index("vocab") == lax.axis_size("vocab") - 1
    source, source_row, slot_index = routing(parents, batch_count, rows_dev)
    picked_slots = jnp.logical_and(
        (source == my_index)[:, :, None],
        slot_index[:, :, None] == jnp.arange(capacity)[None, None, :],
    )
    send_rows = jnp.sum(jnp.where(picked_slots, source_row[:, :, None], 0), axis=1).reshape(-1)
    keys_out = jnp.take(key_cache, send_rows, axis=0).reshape(
        batch_count, capacity, positions, kv_cols
    )
    values_out = jnp.take(value_cache, send_rows, axis=0).reshape(
        batch_count, capacity, positions, kv_cols
    )
    keys_moved, values_moved = (
        lax.all_to_all(keys_out, "batch", split_axis=0, concat_axis=0, tiled=True),
        lax.all_to_all(values_out, "batch", split_axis=0, concat_axis=0, tiled=True),
    )
    own_source = lax.dynamic_index_in_dim(source, my_index, 0, keepdims=False)
    own_slot = lax.dynamic_index_in_dim(slot_index, my_index, 0, keepdims=False)
    arrival = own_source * capacity + own_slot
    next_keys = jnp.take(
        keys_moved.reshape(batch_count * capacity, positions, kv_cols), arrival, axis=0
    )
    next_keys = next_keys.at[:, positions - 1, :].set(
        jnp.where(holds_last, key_new, next_keys[:, positions - 1, :])
    )
    next_values = jnp.take(
        values_moved.reshape(batch_count * capacity, positions, kv_cols), arrival, axis=0
    )
    next_values = next_values.at[:, positions - 1, :].set(
        jnp.where(holds_last, value_new, next_values[:, positions - 1, :])
    )
    attended = attend(queries, next_keys, next_values)
    terms = jnp.dot(
        lax.all_gather(attended, "batch", axis=0, tiled=True),
        out_weight,
        preferred_element_type=jnp.float32,
    )
    total_sum = lax.psum(terms, "vocab")
    residual = hidden.astype(jnp.float32) + total_sum
    squares = lax.psum(jnp.sum(residual * residual, axis=1), "batch")
    normed = (residual * lax.rsqrt(squares[:, None] / D + 1e-05) * final_gain).astype(jnp.bfloat16)
    logits = lax.dot_general(
        lax.all_gather(normed, "batch", axis=1, tiled=True),
        head_weight,
        (((1,), (1,)), ((), ())),
        preferred_element_type=jnp.float32,
    )
    largest = lax.pmax(jnp.max(logits, axis=1), ("batch", "vocab"))
    exp_sum = lax.psum(jnp.sum(jnp.exp(logits - largest[:, None]), axis=1), ("batch", "vocab"))
    log_total = largest + jnp.log(exp_sum)
    vocab_width = past_scores.shape[1]
    local_token = tokens - lax.axis_index(("batch", "vocab")) * vocab_width
    parent_rows = jnp.take(past_scores, parents, axis=0)
    matches = jnp.arange(vocab_width)[None, :] == local_token[:, None]
    picked_score = jnp.sum(jnp.where(matches, parent_rows, 0.0), axis=1)
    beam_score = lax.psum(picked_score, ("batch", "vocab"))
    candidates = beam_score[:, None] + (logits - log_total[:, None])
    return (next_keys, next_values, candidates)


def solution(mesh):
    in_specs = (
        P("batch", None),
        P("batch", None),
        P("batch", None),
        P("batch", "vocab", None),
        P("batch", "vocab", None),
        P(),
        P(),
        P(None, "batch"),
        P("vocab", "batch"),
        P("batch"),
        P(("batch", "vocab"), None),
        P(None, ("batch", "vocab")),
    )
    out_specs = (P("batch", "vocab", None), P("batch", "vocab", None), P(None, ("batch", "vocab")))
    return jax.shard_map(body, mesh=mesh, in_specs=in_specs, out_specs=out_specs, check_vma=False)
```

profile of v0, /device:TPU:1, one launch (start us, length us, event | category | flops | bytes accessed | tf_op | source)
XLA Modules:
  0.0 621.7 jit_solution(4526000379571999110)
XLA Ops:
  9.9 2.0 gather_fusion.1
  11.9 3.4 broadcast_select_fusion
  15.3 60.9 %all_to_all.10 = bf16[16,4,16,1024]{3,2,1,0:T(8,128)(2,1)} all-to-all(bf16[16,4,16,1024]{3,2,1,0:T(8,128)(2,1)S(1)} %bitcast.62), channel_id=1, replica_groups=mesh['batch'=16,'vocab'=16] {'batch'}, dimensions={0} | all-to-all | bytes 4194304 | tf_op jit(solution)/shard_map/all_to_all | solution.py:95
  76.2 4.5 all-to-all-start.1
  81.7 1.4 copy.119
  83.2 2.2 gather_fusion.2
  85.4 42.9 %all-to-all-done.1 = bf16[16,4,16,1024]{3,2,1,0:T(8,128)(2,1)} async-done(((bf16[16,4,16,1024]{3,2,1,0:T(8,128)(2,1)}), bf16[16,4,16,1024]{3,2,1,0:T(8,128)(2,1)}, u32[]{:S(2)}, u32[]{:S(2)}) %all-to-all-start.1) | async-done | bytes 2097184 | tf_op jit(solution)/shard_map/all_to_all | solution.py:96
  128.2 2.2 gather_fusion.4
  133.1 20.5 %all-gather = f32[256,8,8]{2,1,0:T(8,128)S(1)} all-gather(f32[16,8,8]{2,1,0:T(8,128)S(1)} %get-tuple-element.230), channel_id=2, replica_groups=mesh['batch'=16,'vocab'=16] {'vocab'}, dimensions={0}, use_global_device_ids=true | all-gather | bytes 69632 | tf_op jit(solution)/shard_map/all_gather | solution.py:13
  154.4 18.0 %all-gather.1 = f32[256,8,8]{2,1,0:T(8,128)S(1)} all-gather(f32[16,8,8]{2,1,0:T(8,128)S(1)} %exponential_reduce_fusion), channel_id=3, replica_groups=mesh['batch'=16,'vocab'=16] {'vocab'}, dimensions={0}, use_global_device_ids=true | all-gather | bytes 69632 | tf_op jit(solution)/shard_map/all_gather | solution.py:13
  173.6 12.3 %while.19 = (s32[]{:T(128)}, f32[16,8,8]{0,2,1:T(8,128)S(1)}, f32[16,8,8]{0,2,1:T(8,128)S(1)}, f32[16,16,8,8]{1,3,2,0:T(8,128)S(1)}, f32[16,16,8,8]{1,3,2,0:T(8,128)}, /*index=5*/s32[]{:T(128)}, s32[]{:T(128)}, s32[]{:T(128)}) while((s32[]{:T(128)}, f32[16,8,8]{0,2,1:T(8,128)S(1)}, f32[16,8,8]{0,2,1:T(8,128)S(1)}, ...), condition=%wide.region_7.10_spmd, body=%wide.region_6.9_spmd.sunk | while | flops 6149 | bytes 24699 | solution.py:18
  186.1 1.5 fusion.5
  187.6 2.6 copy.129
  190.2 3.6 copy.130
  193.8 82.7 %reduce-scatter.2.cloned.1.call-done = f32[16,512]{1,0:T(8,128)} async-done(((f32[16,8192]{1,0:T(8,128)}), f32[16,512]{1,0:T(8,128)}) %reduce-scatter.2.cloned.1.call-update) | async-done | bytes 32784 | tf_op jit(solution)/shard_map/reduce_scatter | solution.py:57
  277.3 20.4 %all_gather.22 = bf16[256,512]{1,0:T(8,128)(2,1)S(1)} all-gather(bf16[16,512]{1,0:T(8,128)(2,1)S(1)} %convert_element_type.18), channel_id=1, replica_groups=mesh['batch'=16,'vocab'=16] {'batch'}, dimensions={0}, use_global_device_ids=true | all-gather | bytes 278528 | tf_op jit(solution)/shard_map/all_gather | solution.py:115
  298.9 90.3 %all-reduce.3.cloned.1.call-done = f32[256,512]{1,0:T(8,128)} async-done(((f32[256,512]{1,0:T(8,128)}), f32[256,512]{1,0:T(8,128)}) %all-reduce.3.cloned.1.call-update) | async-done | bytes 524304 | tf_op jit(solution)/shard_map/psum | solution.py:119
  389.2 1.2 multiply_reduce_fusion
  390.4 25.4 %psum.30 = f32[256]{0:T(256)S(1)} all-reduce(f32[256]{0:T(256)S(1)} %multiply_reduce_fusion), channel_id=1, replica_groups=mesh['batch'=16,'vocab'=16] {'batch'}, use_global_device_ids=true, to_apply=%region_11.14 | all-reduce | flops 256 | bytes 2048 | tf_op jit(solution)/shard_map/psum | solution.py:121
  415.7 1.9 multiply_convert_fusion
  419.1 40.1 %all-gather.4.cloned.1.call-done = bf16[256,8192]{1,0:T(8,128)(2,1)} async-done(((bf16[256,512]{1,0:T(8,128)(2,1)}), bf16[256,8192]{1,0:T(8,128)(2,1)}) %all-gather.4.cloned.1.call-update) | async-done | bytes 4194320 | tf_op jit(solution)/shard_map/all_gather | solution.py:124
  459.3 6.3 %fusion.16 = (f32[256]{0:T(256)S(1)}, f32[256,501]{0,1:T(8,128)S(1)}) fusion(bf16[256,8192]{1,0:T(8,128)(2,1)} %all-gather.4.cloned.1.call-done, bf16[501,8192]{1,0:T(8,128)(2,1)} %param.32), kind=kOutput, calls=%fused_computation.63 | convolution fusion | flops 2101474304 | bytes 12916736 | tf_op jit(solution)/shard_map/dot_general | solution.py:123
  465.5 76.3 %pmax.7 = f32[256]{0:T(256)S(1)} all-reduce(f32[256]{0:T(256)S(1)} %get-tuple-element.232), channel_id=1, replica_groups=mesh['batch'=16,'vocab'=16] {'batch','vocab'}, use_global_device_ids=true, to_apply=%region_13.16 | all-reduce | flops 256 | bytes 2048 | tf_op jit(solution)/shard_map/pmax | solution.py:129
  542.0 72.3 %all-reduce = (f32[256]{0:T(256)S(1)}, f32[256]{0:T(256)S(1)}) all-reduce(f32[256]{0:T(256)S(1)} %exponential_reduce_fusion.1, f32[256]{0:T(256)S(1)} %select_reduce_fusion), channel_id=1, replica_groups=mesh['batch'=16,'vocab'=16] {'batch','vocab'}, use_global_device_ids=true, to_apply=%region_15.18 | all-reduce | flops 512 | bytes 4096 | tf_op jit(solution)/shard_map/psum | solution.py:130
  (93 shorter events, 24.9 us)
Async XLA Ops:
  7.2 1.7 copy-start
  8.9 1.0 copy-start.1
  76.2 4.5 copy-start.7
  76.2 52.1 %all-to-all-start.1 = ((bf16[16,4,16,1024]{3,2,1,0:T(8,128)(2,1)}), bf16[16,4,16,1024]{3,2,1,0:T(8,128)(2,1)}, u32[]{:S(2)}, u32[]{:S(2)}) async-start(bf16[16,4,16,1024]{3,2,1,0:T(8,128)(2,1)} %bitcast.6), calls=%async_computation.1 | async-start | bytes 4194304 | tf_op jit(solution)/shard_map/all_to_all | solution.py:96
  80.6 195.9 %reduce-scatter.2.cloned.1.call-start = ((), (), s32[]{:S(2)}) async-start(), calls=%async_computation.3 | async-start | bytes 557056 | tf_op jit(solution)/shard_map/reduce_scatter | solution.py:57
  83.2 47.5 %copy-start.8 = (bf16[16,1024]{1,0:T(8,128)(2,1)S(1)}, bf16[16,1024]{1,0:T(8,128)(2,1)}, u32[]{:S(2)}) copy-start(bf16[16,1024]{1,0:T(8,128)(2,1)} %param.24) | copy-start | bytes 98308
  85.4 46.0 %copy-start.9 = (bf16[16,1024]{1,0:T(8,128)(2,1)S(1)}, bf16[16,1024]{1,0:T(8,128)(2,1)}, u32[]{:S(2)}) copy-start(bf16[16,1024]{1,0:T(8,128)(2,1)} %param.23) | copy-start | bytes 98308
  131.3 0.8 copy-start.4
  132.6 21.8 %copy-start.2 = (bf16[16,16,1024]{2,1,0:T(8,128)(2,1)}, bf16[16,16,1024]{2,1,0:T(8,128)(2,1)S(1)}, u32[]{:S(2)}) copy-start(bf16[16,16,1024]{2,1,0:T(8,128)(2,1)S(1)} %scatter.6) | copy-start | bytes 1572868
  190.2 107.5 %copy-start.5 = (bf16[512,512]{1,0:T(8,128)(2,1)S(1)}, bf16[512,512]{1,0:T(8,128)(2,1)}, u32[]{:S(2)}) copy-start(bf16[512,512]{1,0:T(8,128)(2,1)} %param.30) | copy-start | bytes 1572868
  193.7 195.5 %copy-start.3 = (bf16[256,512]{1,0:T(8,128)(2,1)S(1)}, bf16[256,512]{1,0:T(8,128)(2,1)}, u32[]{:S(2)}) copy-start(bf16[256,512]{1,0:T(8,128)(2,1)} %param.29) | copy-start | bytes 786436
  193.7 222.0 %copy-start.11 = (f32[512]{0:T(512)S(1)}, f32[512]{0:T(512)}, u32[]{:S(2)}) copy-start(f32[512]{0:T(512)} %param.31) | copy-start | bytes 6148
  193.8 195.4 %all-reduce.3.cloned.1.call-start = ((), (), s32[]{:S(2)}) async-start(), calls=%async_computation.4 | async-start | bytes 1048576 | tf_op jit(solution)/shard_map/psum | solution.py:119
  277.3 140.3 %copy-start.6 = (f32[256,501]{0,1:T(8,128)S(1)}, f32[256,501]{0,1:T(8,128)}, u32[]{:S(2)}) copy-start(f32[256,501]{0,1:T(8,128)} %param.33) | copy-start | bytes 1539076
  298.8 119.1 %copy-start.10 = (s32[256]{0:T(256)S(1)}, s32[256]{0:T(256)}, u32[]{:S(2)}) copy-start(s32[256]{0:T(256)} %param.27) | copy-start | bytes 3076
  298.8 160.5 %all-gather.4.cloned.1.call-start = ((), (), s32[]{:S(2)}) async-start(), calls=%async_computation.5 | async-start | bytes 4456448 | tf_op jit(solution)/shard_map/all_gather | solution.py:124
  417.9 1.0 copy-start.12
Sparse Core Ops, SparseCore 0:
  193.9 82.6 reduce-scatter.1
  298.9 90.2 all-reduce.2
  417.8 41.4 all-gather.3
where the time goes:
time: 623 us; the launch traced here: 622 us
  blocking collectives  294 us (47%)
  waiting for transfers between devices  256 us (41%)
  local copies, waits for them, and re-layouts  21.9 us (4%)
  other arithmetic  21.6 us (3%)
  between operations  14.2 us (2%)
  matrix products  9.35 us (2%)
    psum x1, waiting for transfers between devices, body(): total_sum = lax.psum(terms, 'vocab')  90.3 us
    reduce_scatter x1, waiting for transfers between devices, attend(): lax.psum_scatter(mixture.reshape(row_count, -1), 'vocab', scatter_dimensi...  82.7 us
    pmax x1, blocking collectives, body(): largest = lax.pmax(jnp.max(logits, axis=1), ('batch', 'vocab'))  76.3 us
    psum x1, blocking collectives, body(): lax.psum(jnp.sum(jnp.exp(logits - largest[:, None]), axis=1), ('batch', '...  72.3 us
    all_to_all x1, blocking collectives, body(): lax.all_to_all(keys_out, 'batch', split_axis=0, concat_axis=0, tiled=True)  60.9 us
    all_to_all x1, waiting for transfers between devices, body(): lax.all_to_all(values_out, 'batch', split_axis=0, concat_axis=0, tiled=True)  42.9 us
    all_gather x1, waiting for transfers between devices, body(): lax.all_gather(normed, 'batch', axis=1, tiled=True)  40.1 us
    all_gather x2, blocking collectives, joined(): gathered = jax.tree.map(lambda a: lax.all_gather(a, axis), part)  38.5 us
  transfers between devices with their start and end apart: 4, of which 4 were waited for; matrix products, arithmetic and copies ran while one was open for 1% of the time, Pallas kernels for 0%

commit v1 on v0

v1 whole, which is shorter than its diff:
```python
import functools

import jax
import jax.numpy as jnp
from jax import lax
from jax.experimental import pallas as pl
from jax.experimental.pallas import tpu as pltpu
from jax.sharding import PartitionSpec as P

D = 8192
HEAD_DIM = 128
MESH = pl.DeviceIdType.MESH
F32 = jnp.float32
BF16 = jnp.bfloat16
NT = (((1,), (1,)), ((), ()))

BULK_EARLY_K = (1, 7, 2, 6, 4)
BULK_EARLY_V = ()
BULK_LATE_K = (3, 5)
BULK_LATE_V = (1, 7, 2, 6, 3, 5, 4)


def iota(shape, axis):
    return lax.broadcasted_iota(jnp.int32, shape, axis)


def kernel(
    q_ref, kn_ref, vn_ref, kc_ref, vc_ref, par_ref, tok_ref, hid_ref, w_ref, gain_ref, hw_ref, past_ref,
    nk_ref, nv_ref, cand_ref,
    q_v, kn_v, vn_v, kc_v, vc_v, hid_v, w_v, hw_v, past_v,
    kt, vt, xs, xr, perm, qp, kn_s, vn_s, o_s, rs, ar, a_s, aa, ps, pr,
    ks, vs, kr, vr, nb, sq_s, sq_r, sc_s, sc_r, acc, pick, lv_s, lv_r, lb_s, lb_r,
    lsem, rsem, ssem, s1, s2, t1, t2,
):
    b = lax.axis_index("batch")
    v = lax.axis_index("vocab")
    z, c = b // 2, b % 2
    kind = (c + z) % 2
    g, h = v // 2, v % 2
    x, y = v // 4, v % 4

    def same_kind(zz):
        return 2 * zz + (kind + zz) % 2

    def send(src, dst, send_sem, recv_sem, dev):
        pltpu.make_async_remote_copy(
            src_ref=src, dst_ref=dst, send_sem=send_sem, recv_sem=recv_sem,
            device_id=dev, device_id_type=MESH,
        ).start()

    def wait(ref, sem):
        pltpu.make_async_copy(ref, ref, sem).wait()

    local = [
        pltpu.make_async_copy(q_ref.at[:, pl.ds(pl.multiple_of(g * 1024, 1024), 1024)], q_v, lsem.at[0]),
        pltpu.make_async_copy(kn_ref, kn_v, lsem.at[1]),
        pltpu.make_async_copy(vn_ref, vn_v, lsem.at[2]),
        pltpu.make_async_copy(kc_ref, kc_v, lsem.at[3]),
        pltpu.make_async_copy(vc_ref, vc_v, lsem.at[4]),
        pltpu.make_async_copy(past_ref, past_v, lsem.at[5]),
        pltpu.make_async_copy(w_ref, w_v, lsem.at[6]),
        pltpu.make_async_copy(hid_ref.at[pl.ds(pl.multiple_of(v * 16, 16), 16)], hid_v, lsem.at[7]),
        pltpu.make_async_copy(hw_ref, hw_v, lsem.at[8]),
    ]
    for copy in local:
        copy.start()

    bar = pltpu.get_barrier_semaphore()

    def greet(d, _):
        pl.semaphore_signal(bar, inc=1, device_id=(b, (v + d) % 16), device_id_type=MESH)
        pl.semaphore_signal(bar, inc=1, device_id=((b + d) % 16, v), device_id_type=MESH)
        pl.semaphore_signal(bar, inc=1, device_id=((b + d) % 16, 2 * g + 1 - h), device_id_type=MESH)
        return 0

    lax.fori_loop(1, 16, greet, 0)

    for copy in local[:3]:
        copy.wait()
    lane_g = pl.ds(pl.multiple_of(g * 128, 128), 128)
    packed = jnp.concatenate(
        [q_v[...].astype(F32), kn_v[:, lane_g].astype(F32), vn_v[:, lane_g].astype(F32)], axis=1
    )
    upper = h.astype(F32)
    packed = packed[0:8] * (1.0 - upper) + packed[8:16] * upper
    packed = jnp.concatenate([packed[:, :640], packed[:, 640:]], axis=0).astype(BF16)
    xs[...] = packed
    xr[z] = packed

    pl.semaphore_wait(bar, 45)

    def send_query(d, _):
        zz = (z + d) % 8
        send(xs, xr.at[z], ssem.at[0], rsem.at[0], (same_kind(zz), v))
        return 0

    lax.fori_loop(1, 8, send_query, 0)

    def cache_part(ref, target):
        rows = pl.ds(pl.multiple_of((target % 2) * 8, 8), 8)
        return ref.at[rows, :, pl.ds(pl.multiple_of((target // 2) * 128, 128), 128)]

    my_pos = pl.ds(pl.multiple_of(v * 16, 16), 16)

    def turn(ref, out, i):
        def step(d, _):
            t = (v + d) % 16
            send(cache_part(ref, t), out.at[:, my_pos, :], ssem.at[i], rsem.at[i], (b, t))
            return 0

        lax.fori_loop(1, 16, step, 0)
        pltpu.make_async_copy(cache_part(ref, v), out.at[:, my_pos, :], rsem.at[i]).start()

    turn(kc_ref, kt, 1)
    turn(vc_ref, vt, 2)

    local[3].wait()
    local[4].wait()

    def stage(zz, _):
        base = same_kind(zz) * 16
        count = jnp.int32(0)
        rows = [jnp.int32(0)] * 4
        for r in range(16):
            mine = (par_ref[base + r] // 32 == z).astype(jnp.int32)
            for k in range(4):
                rows[k] = jnp.where(count * mine + mine == k + 1, r, rows[k])
            count = count + mine
        for k in range(4):
            ks[zz, k] = kc_v[rows[k]]
            vs[zz, k] = vc_v[rows[k]]
        return 0

    lax.fori_loop(0, 8, stage, 0)
    kr[z] = ks[z]
    vr[z] = vs[z]

    def bulk(src, dst, i, distances):
        for d in distances:
            zz = (z + d) % 8
            send(src.at[zz], dst.at[z], ssem.at[i], rsem.at[i], (same_kind(zz), v))

    bulk(ks, kr, 3, BULK_EARLY_K)
    bulk(vs, vr, 4, BULK_EARLY_V)

    lanes = iota((128, 1024), 1)
    wanted = (lanes % 128) * 8 + lanes // 128
    subs = iota((128, 1024), 0)

    def build(t, _):
        perm[pl.ds(pl.multiple_of(t * 128, 128), 128), :] = (subs + t * 128 == wanted).astype(F32).astype(BF16)
        return 0

    lax.fori_loop(0, 8, build, 0)
    k64 = iota((64, 64), 0)
    swap = (iota((64, 64), 1) == (k64 % 8) * 8 + k64 // 8).astype(F32).astype(BF16)

    local[5].wait()
    first_token = (b * 16 + v) * 501
    lane501 = iota((1, 501), 1)

    def pick_row(i, _):
        row = past_v[pl.ds(par_ref[i], 1), :]
        hit = jnp.where(lane501 == tok_ref[i] - first_token, row, 0.0)
        pick[pl.ds(i, 1), :] = jnp.sum(hit, axis=1, keepdims=True)
        return 0

    lax.fori_loop(0, 256, pick_row, 0)

    wait(xr.at[0:7], rsem.at[0])
    got = xr[...].astype(F32)
    got = jnp.concatenate(
        [got[:, 0:8, :].reshape(64, 640), got[:, 8:16, :].reshape(64, 640)], axis=1
    ).astype(BF16)
    got = jnp.dot(swap, got, preferred_element_type=F32)
    kn_s[...] = got[:, 1024:1152]
    vn_s[...] = got[:, 1152:1280]
    qp[...] = jnp.dot(got[:, :1024].astype(BF16), perm[...], preferred_element_type=F32)
    wait(kt, rsem.at[1])
    wait(vt, rsem.at[2])
    lane256 = iota((64, 256), 1)

    def attend(r, _):
        rows = pl.ds(pl.multiple_of(r * 8, 8), 8)
        qr = qp[rows, :]
        qf = jnp.concatenate([qr[:, j * 128:(j + 1) * 128] for j in range(8)], axis=0)
        new_key = jnp.concatenate([kn_s[rows, :]] * 8, axis=0)
        new_value = jnp.concatenate([vn_s[rows, :]] * 8, axis=0)
        s = lax.dot_general(qf.astype(BF16), kt[r], NT, preferred_element_type=F32)
        s_new = jnp.sum(qf * new_key, axis=1, keepdims=True)
        s = jnp.where(lane256 == 255, s_new, s) * HEAD_DIM ** (-0.5)
        e = jnp.exp(s - jnp.max(s, axis=1, keepdims=True))
        wf = (e / jnp.sum(e, axis=1, keepdims=True)).astype(BF16).astype(F32)
        w_new = wf[:, 255:256]
        w_old = jnp.where(lane256 == 255, 0.0, wf).astype(BF16)
        o = jnp.dot(w_old, vt[r], preferred_element_type=F32) + w_new * new_value
        o_s[rows, :] = jnp.concatenate([o[j * 8:(j + 1) * 8] for j in range(8)], axis=1)
        return 0

    lax.fori_loop(0, 8, attend, 0)
    o = lax.dot_general(o_s[...].astype(BF16), perm[...], NT, preferred_element_type=F32).astype(BF16)
    o = jnp.dot(swap, o, preferred_element_type=F32).reshape(8, 8, 1024)
    rs[...] = jnp.concatenate([o[:, :, :512], o[:, :, 512:]], axis=1).astype(BF16)
    ar[z] = rs[z]

    def send_back(d, _):
        zz = (z + d) % 8
        send(rs.at[zz], ar.at[z], ssem.at[5], rsem.at[5], (same_kind(zz), v))
        return 0

    lax.fori_loop(1, 8, send_back, 0)
    sub16 = iota((16, 512), 0)
    beam = jnp.zeros((16, 512), jnp.int32)
    for r in range(8):
        beam = jnp.where(sub16 % 8 == r, par_ref[b * 16 + h * 8 + r] // 32, beam)
    wait(ar.at[0:7], rsem.at[5])
    att = jnp.zeros((16, 512), F32)
    for p in range(8):
        att = jnp.where(beam == p, ar[p].astype(F32), att)
    for hh in range(2):
        part = att[hh * 8:hh * 8 + 8]
        a_s[hh] = jnp.concatenate([part[:, :256], part[:, 256:]], axis=0).astype(BF16)
    aa[2 * b + h] = a_s[h]

    slot = aa.at[2 * b + h]
    send(a_s.at[1 - h], slot, ssem.at[6], rsem.at[6], (b, 2 * g + 1 - h))

    def spread(d, _):
        for hh in range(2):
            send(a_s.at[hh], slot, ssem.at[6], rsem.at[6], ((b + d) % 16, 2 * g + hh))
        return 0

    lax.fori_loop(1, 16, spread, 0)
    local[6].wait()
    local[7].wait()
    wait(aa.at[0:31], rsem.at[6])
    rows_in = aa[...].astype(F32)
    rows_in = jnp.concatenate(
        [rows_in[:, 0:8, :].reshape(256, 256), rows_in[:, 8:16, :].reshape(256, 256)], axis=1
    ).astype(BF16)
    ps[...] = jnp.dot(rows_in, w_v[...], preferred_element_type=F32).astype(BF16).reshape(16, 16, 512)
    pr[v] = ps[v]

    def send_partial(d, _):
        t = (v + d) % 16
        send(ps.at[t], pr.at[v], ssem.at[7], rsem.at[7], (b, t))
        return 0

    lax.fori_loop(1, 16, send_partial, 0)
    wait(pr.at[0:15], rsem.at[7])
    residual = hid_v[...].astype(F32) + jnp.sum(pr[...].astype(F32), axis=0)
    nb[c, v, z] = (residual * gain_ref[...]).astype(BF16)

    def send_state(d, _):
        zz = (z + d) % 8
        send(nb.at[c, v, z], nb.at[c, v, z], ssem.at[8], rsem.at[8], (2 * zz + c, v))
        return 0

    lax.fori_loop(1, 8, send_state, 0)
    diag16 = iota((16, 128), 0) == iota((16, 128), 1)
    square = jnp.sum(residual * residual, axis=1, keepdims=True)
    square = jnp.sum(jnp.where(diag16, square, 0.0), axis=0, keepdims=True)
    sq_s[...] = square
    sq_r[b] = square

    def send_square(d, _):
        send(sq_s, sq_r.at[b], ssem.at[9], rsem.at[9], ((b + d) % 16, v))
        return 0

    lax.fori_loop(1, 16, send_square, 0)
    wait(nb.at[0, 0, 0:7], rsem.at[8])

    def along(u, axis, d):
        if axis == 0:
            return ((u // 4 + d) % 4) * 4 + u % 4
        return (u // 4) * 4 + (u % 4 + d) % 4

    def piece(u, half, part=None):
        if part is None:
            return nb.at[c, u, 4 * half:4 * half + 4]
        return nb.at[c, u, 4 * half + 2 * part:4 * half + 2 * part + 2]

    def state(ref, axis, d, sem):
        send(ref, ref, ssem.at[10], sem, (b, along(v, axis, d)))

    def sibling(ref):
        send(ref, ref, ssem.at[11], rsem.at[10], (2 * z + 1 - c, v))

    halves = ((1, 0), (0, 1))

    def first(half, order=halves):
        axis = order[half][0]
        state(piece(v, half), axis, 1, s1.at[half, 0])
        state(piece(v, half), axis, -1, s1.at[half, 1])

    def second(half, o):
        u = along(v, halves[half][0], o)
        axis = halves[half][1]
        state(piece(u, half), axis, 1, t1.at[half, o, 0])
        state(piece(u, half), axis, -1, t1.at[half, o, 1])

    def second_forward(half, o):
        u = along(v, halves[half][0], o)
        axis = halves[half][1]
        wait(piece(u, half), t1.at[half, o, 0])
        state(piece(along(u, axis, -1), half, 0), axis, 1, t2.at[half, o, 0])
        sibling(piece(along(u, axis, -1), half))
        wait(piece(u, half), t1.at[half, o, 1])
        state(piece(along(u, axis, 1), half, 1), axis, -1, t2.at[half, o, 1])
        sibling(piece(along(u, axis, 1), half))

    for half in range(2):
        first(half)
    for half in range(2):
        second(half, 0)
        sibling(piece(v, half))
    for half in range(2):
        axis = halves[half][0]
        wait(piece(v, half), s1.at[half, 0])
        state(piece(along(v, axis, -1), half, 0), axis, 1, s2.at[half, 0])
        wait(piece(v, half), s1.at[half, 1])
        state(piece(along(v, axis, 1), half, 1), axis, -1, s2.at[half, 1])
    for half in range(2):
        second(half, 3)
        second(half, 1)
        sibling(piece(along(v, halves[half][0], -1), half))
        sibling(piece(along(v, halves[half][0], 1), half))
    bulk(ks, kr, 3, BULK_LATE_K)
    bulk(vs, vr, 4, BULK_LATE_V)
    for half in range(2):
        second_forward(half, 0)
    for half in range(2):
        wait(piece(v, half, 0), s2.at[half, 0])
        wait(piece(v, half, 1), s2.at[half, 1])
        second(half, 2)
        sibling(piece(along(v, halves[half][0], 2), half))

    wait(sq_r.at[0:15], rsem.at[9])
    scale = lax.rsqrt(jnp.sum(sq_r[...], axis=0) / D + 1e-05)
    sc_s[...] = scale
    sc_r[v] = scale

    def send_scale(d, _):
        send(sc_s, sc_r.at[v], ssem.at[12], rsem.at[11], (b, (v + d) % 16))
        return 0

    lax.fori_loop(1, 16, send_scale, 0)
    for o in (3, 1, 2):
        for half in range(2):
            second_forward(half, o)
    for o in (0, 3, 1, 2):
        for half in range(2):
            u = along(v, halves[half][0], o)
            axis = halves[half][1]
            wait(piece(u, half, 0), t2.at[half, o, 0])
            wait(piece(u, half, 1), t2.at[half, o, 1])
            sibling(piece(along(u, axis, 2), half))

    local[8].wait()

    def product(core, zz):
        cols = pl.ds(pl.multiple_of((2 * zz + core) * 512, 512), 512)
        return lax.dot_general(
            nb[core, :, zz].reshape(256, 512), hw_v[:, cols], NT, preferred_element_type=F32
        )

    acc[...] = product(c, 0)

    def own_share(zz, _):
        acc[...] += product(c, zz)
        return 0

    lax.fori_loop(1, 8, own_share, 0)
    wait(nb.at[0], rsem.at[10])

    def other_share(zz, _):
        acc[...] += product(1 - c, zz)
        return 0

    lax.fori_loop(0, 8, other_share, 0)
    wait(sc_r.at[0:15], rsem.at[11])
    diag3 = iota((16, 16, 128), 1) == iota((16, 16, 128), 2)
    scales = jnp.sum(jnp.where(diag3, sc_r[...], 0.0), axis=2, keepdims=True).reshape(256, 1)
    logits = acc[...] * scales
    acc[...] = logits
    largest = jnp.max(logits, axis=1, keepdims=True)
    total = jnp.sum(jnp.exp(logits - largest), axis=1, keepdims=True)
    diag128 = iota((128, 128), 0) == iota((128, 128), 1)

    def to_rows(column):
        parts = [
            jnp.sum(jnp.where(diag128, column[k * 128:(k + 1) * 128], 0.0), axis=0, keepdims=True)
            for k in range(2)
        ]
        return jnp.concatenate(parts, axis=0)

    def to_column(rows):
        parts = [
            jnp.sum(jnp.where(diag128, rows[k:k + 1], 0.0), axis=1, keepdims=True) for k in range(2)
        ]
        return jnp.concatenate(parts, axis=0)

    def merged(stats):
        high = jnp.max(stats[:, 0:2], axis=0)
        return jnp.concatenate(
            [
                high,
                jnp.sum(stats[:, 2:4] * jnp.exp(stats[:, 0:2] - high), axis=0),
                jnp.sum(stats[:, 4:6], axis=0),
                jnp.zeros((2, 128), F32),
            ],
            axis=0,
        )

    stats = jnp.concatenate(
        [to_rows(largest), to_rows(total), to_rows(pick[...]), jnp.zeros((2, 128), F32)], axis=0
    )
    lv_s[...] = stats
    lv_r[v] = stats

    def send_vocab(d, _):
        send(lv_s, lv_r.at[v], ssem.at[13], rsem.at[12], (b, (v + d) % 16))
        return 0

    lax.fori_loop(1, 16, send_vocab, 0)
    wait(lv_r.at[0:15], rsem.at[12])
    stats = merged(lv_r[...])
    lb_s[...] = stats
    lb_r[b] = stats

    def send_batch(d, _):
        send(lb_s, lb_r.at[b], ssem.at[14], rsem.at[13], ((b + d) % 16, v))
        return 0

    lax.fori_loop(1, 16, send_batch, 0)

    wait(kr.at[0:7], rsem.at[3])
    wait(vr.at[0:7], rsem.at[4])
    last = iota((16, 1024), 0) == jnp.where(v == 15, 15, 99)
    new_keys = kn_v[...].astype(F32)
    new_values = vn_v[...].astype(F32)
    beams = [par_ref[b * 16 + r] // 32 for r in range(16)]
    for r in range(16):
        at = jnp.int32(0)
        for earlier in range(r):
            at = at + (beams[earlier] == beams[r]).astype(jnp.int32)
        at = jnp.minimum(at, 3)
        nk_ref[r] = jnp.where(last, new_keys[r:r + 1], kr[beams[r], at].astype(F32)).astype(BF16)
        nv_ref[r] = jnp.where(last, new_values[r:r + 1], vr[beams[r], at].astype(F32)).astype(BF16)

    wait(lb_r.at[0:15], rsem.at[13])
    stats = merged(lb_r[...])
    offset = stats[4:6] - (stats[0:2] + jnp.log(stats[2:4]))
    cand_ref[...] = acc[...] + to_column(offset)

    wait(xr.at[0:7], ssem.at[0])
    wait(kt.at[:, 0:240], ssem.at[1])
    wait(vt.at[:, 0:240], ssem.at[2])
    wait(kr.at[0:7], ssem.at[3])
    wait(vr.at[0:7], ssem.at[4])
    wait(ar.at[0:7], ssem.at[5])
    wait(aa.at[0:31], ssem.at[6])
    wait(pr.at[0:15], ssem.at[7])
    wait(nb.at[0, 0, 0:7], ssem.at[8])
    wait(sq_r.at[0:15], ssem.at[9])
    wait(nb.at[0, 0:15], ssem.at[10])
    wait(nb.at[0], ssem.at[11])
    wait(sc_r.at[0:15], ssem.at[12])
    wait(lv_r.at[0:15], ssem.at[13])
    wait(lb_r.at[0:15], ssem.at[14])


def body(
    queries, key_new, value_new, key_cache, value_cache, parents, tokens, hidden, out_weight, final_gain,
    head_weight, past_scores,
):
    any_space = pl.BlockSpec(memory_space=pl.ANY)
    vmem = pl.BlockSpec(memory_space=pltpu.VMEM)
    smem = pl.BlockSpec(memory_space=pltpu.SMEM)
    V = pltpu.VMEM
    scratch = [
        V((16, 1024), BF16), V((16, 1024), BF16), V((16, 1024), BF16),
        V((16, 16, 1024), BF16), V((16, 16, 1024), BF16),
        V((16, 512), BF16), V((512, 512), BF16), V((501, 8192), BF16), V((256, 501), F32),
        V((8, 256, 128), BF16), V((8, 256, 128), BF16),
        V((16, 640), BF16), V((8, 16, 640), BF16), V((1024, 1024), BF16),
        V((64, 1024), F32), V((64, 128), F32), V((64, 128), F32), V((64, 1024), F32),
        V((8, 16, 512), BF16), V((8, 16, 512), BF16),
        V((2, 16, 256), BF16), V((32, 16, 256), BF16),
        V((16, 16, 512), BF16), V((16, 16, 512), BF16),
        V((8, 4, 16, 1024), BF16), V((8, 4, 16, 1024), BF16),
        V((8, 4, 16, 1024), BF16), V((8, 4, 16, 1024), BF16),
        V((2, 16, 8, 16, 512), BF16),
        V((1, 128), F32), V((16, 1, 128), F32), V((1, 128), F32), V((16, 1, 128), F32),
        V((256, 501), F32), V((256, 1), F32),
        V((8, 128), F32), V((16, 8, 128), F32), V((8, 128), F32), V((16, 8, 128), F32),
        pltpu.SemaphoreType.DMA((9,)), pltpu.SemaphoreType.DMA((14,)), pltpu.SemaphoreType.DMA((15,)),
        pltpu.SemaphoreType.DMA((2, 2)), pltpu.SemaphoreType.DMA((2, 2)),
        pltpu.SemaphoreType.DMA((2, 4, 2)), pltpu.SemaphoreType.DMA((2, 4, 2)),
    ]
    return pl.pallas_call(
        kernel,
        out_shape=(
            jax.ShapeDtypeStruct((16, 16, 1024), BF16),
            jax.ShapeDtypeStruct((16, 16, 1024), BF16),
            jax.ShapeDtypeStruct((256, 501), F32),
        ),
        in_specs=[any_space] * 5 + [smem] * 2 + [any_space] * 2 + [vmem] + [any_space] * 2,
        out_specs=(vmem, vmem, vmem),
        scratch_shapes=scratch,
        compiler_params=pltpu.CompilerParams(
            collective_id=0, has_side_effects=True, vmem_limit_bytes=48 * 1024 * 1024
        ),
        name="beam_step",
    )(
        queries, key_new, value_new, key_cache, value_cache, parents, tokens, hidden, out_weight,
        final_gain.reshape(1, 512), head_weight, past_scores,
    )


def solution(mesh):
    in_specs = (
        P("batch", None), P("batch", None), P("batch", None),
        P("batch", "vocab", None), P("batch", "vocab", None),
        P(), P(), P(None, "batch"), P("vocab", "batch"), P("batch"),
        P(("batch", "vocab"), None), P(None, ("batch", "vocab")),
    )
    out_specs = (P("batch", "vocab", None), P("batch", "vocab", None), P(None, ("batch", "vocab")))
    return jax.shard_map(body, mesh=mesh, in_specs=in_specs, out_specs=out_specs, check_vma=False)
```

time: 623 us -> 119 us (0.19)
  blocking collectives: 294 us -> 0 us
  waiting for transfers between devices: 256 us -> 0 us
  Pallas kernels: 0 us -> 105 us
  other arithmetic: 21.6 us -> 0 us
  between operations: 14.2 us -> 0.66 us
  local copies, waits for them, and re-layouts: 21.9 us -> 12.4 us
  matrix products: 9.35 us -> 0 us
    pallas_call x0 -> x1, Pallas kernels: none -> 105 us  [body(): pl.pallas_call(kernel, out_shape=(jax.ShapeDtypeStruct((16, 16, 1024), BF...]
    psum x2 -> x0, blocking collectives: 97.7 us -> none  [the longest x1 72.3 us: body(): lax.psum(jnp.sum(jnp.exp(logits - largest[:, None]), axis=1), ('batch', '...]
    psum x1 -> x0, waiting for transfers between devices: 90.3 us -> none  [body(): total_sum = lax.psum(terms, 'vocab')]
    reduce_scatter x1 -> x0, waiting for transfers between devices: 82.7 us -> none  [attend(): lax.psum_scatter(mixture.reshape(row_count, -1), 'vocab', scatter_dimensi...]
    pmax x1 -> x0, blocking collectives: 76.3 us -> none  [body(): largest = lax.pmax(jnp.max(logits, axis=1), ('batch', 'vocab'))]
    all_to_all x1 -> x0, blocking collectives: 60.9 us -> none  [body(): lax.all_to_all(keys_out, 'batch', split_axis=0, concat_axis=0, tiled=True)]
    all_gather x3 -> x0, blocking collectives: 58.8 us -> none  [the longest x2 38.5 us: joined(): gathered = jax.tree.map(lambda a: lax.all_gather(a, axis), part)]
    all_to_all x1 -> x0, waiting for transfers between devices: 42.9 us -> none  [body(): lax.all_to_all(values_out, 'batch', split_axis=0, concat_axis=0, tiled=True)]
  transfers between devices with their start and end apart: 4 -> 0, of which waited for: 4 -> 0; matrix products, arithmetic and copies ran while one was open for 1% -> 0% of each run, Pallas kernels for 0% -> 0%
where the time goes in v1:
time: 119 us; the launch traced here: 118 us
  Pallas kernels  105 us (88%)
  local copies, waits for them, and re-layouts  12.4 us (10%)
    pallas_call x1, Pallas kernels, body(): pl.pallas_call(kernel, out_shape=(jax.ShapeDtypeStruct((16, 16, 1024), BF...  105 us
    unnamed x23, local copies, waits for them, and re-layouts  11.4 us

profile of v1, /device:TPU:1, one launch (start us, length us, event | category | flops | bytes accessed | tf_op | source)
XLA Modules:
  0.0 118.3 jit_solution(18046948010118841358)
XLA Ops:
  0.6 1.2 %copy.15.past_ref = f32[256,501]{1,0:T(8,128)S(1)} copy(f32[256,501]{0,1:T(8,128)} %param.23) | data formatting | bytes 1026048 | tf_op args[11]
  1.9 0.0 copy-start
  1.9 1.0 copy-done
  2.9 0.0 copy-start.1
  2.9 1.0 copy-done.1
  4.0 0.0 copy-start.2
  4.0 1.0 copy-done.2
  5.0 0.0 copy-start.3
  5.0 0.9 copy-done.3
  6.0 0.0 copy-start.4
  6.0 0.9 copy-done.4
  6.9 0.0 copy-start.5
  6.9 0.8 copy-done.5
  7.7 0.0 copy-start.6
  7.7 0.8 copy-done.6
  8.4 0.0 copy-start.7
  8.4 0.7 copy-done.7
  9.1 0.0 copy-start.8
  9.1 0.7 copy-done.8
  9.8 0.7 copy-done.9
  10.5 105.2 %beam_step.1 = (bf16[16,16,1024]{2,1,0:T(8,128)(2,1)S(1)}, bf16[16,16,1024]{2,1,0:T(8,128)(2,1)S(1)}, f32[256,501]{1,0:T(8,128)S(1)}) custom-call(bf16[16,8192]{1,0:T(8,128)(2,1)S(1)} %copy-done.3, bf16[16,1024]{1,0:T(8,128)(2,1)S(1)} %copy-done.5, bf16[16,1024]{1,0:T(8,128)(2,1)S(1)} %copy-done.6, bf16[16,16,1024]{2,1,0:T(8,128)(2,1)S(1)} %copy-done, ...), custom_call_target="tpu_custom_call" | custom-call | tf_op jit(solution)/shard_map/beam_step/pallas_call | solution.py:501
  115.7 1.0 copy.16
  116.7 0.8 copy.19
  117.5 0.8 copy.20
  (1 shorter events, 0.0 us)
Async XLA Ops:
  1.9 1.0 copy-start
  2.9 1.0 copy-start.1
  4.0 1.0 copy-start.2
  5.0 0.9 copy-start.3
  6.0 0.9 copy-start.4
  6.9 0.8 copy-start.5
  7.7 0.8 copy-start.6
  8.4 0.7 copy-start.7
  9.1 0.7 copy-start.8
  9.8 0.7 copy-start.9

commit v2 on v1

v2 whole, which is shorter than its diff:
```python
import functools

import jax
import jax.numpy as jnp
from jax import lax
from jax.experimental import pallas as pl
from jax.experimental.pallas import tpu as pltpu
from jax.sharding import PartitionSpec as P

D = 8192
HEAD_DIM = 128
MESH = pl.DeviceIdType.MESH
F32 = jnp.float32
BF16 = jnp.bfloat16
NT = (((1,), (1,)), ((), ()))

BULK_EARLY_K = (1, 7, 2, 6, 4)
BULK_MID_V = (4,)
BULK_LATE_K = (3, 5)
BULK_LATE_V = (1, 7, 2, 6, 3, 5)
AWAY = (0, 1, 7, 2, 6, 3, 5, 4)


def iota(shape, axis):
    return lax.broadcasted_iota(jnp.int32, shape, axis)


def kernel(
    q_ref, kn_ref, vn_ref, kc_ref, vc_ref, par_ref, pl_ref, tl_ref, hid_ref, w_ref, gain_ref, hw_ref, past_ref,
    nk_ref, nv_ref, cand_ref,
    q_v, kn_v, vn_v, kc_v, vc_v, par_s, par_v, tok_v, hid_v, w_v, gain_v, hw_v, past_v,
    kt, vt, xs, xr, perm, qp, kn_s, vn_s, w_s, o_new, o_s, rs, ar, a_s, aa, ps, pr,
    ks, vs, kr, vr, nb, sq_s, sq_r, sc_s, sc_r, acc, nk_s, nv_s, lv_s, lv_r, lb_s, lb_r,
    lsem, rsem, ssem, s1, s2, t1, t2,
):
    b = lax.axis_index("batch")
    v = lax.axis_index("vocab")
    z, c = b // 2, b % 2
    kind = (c + z) % 2
    g, h = v // 2, v % 2
    x, y = v // 4, v % 4

    def same_kind(zz):
        return 2 * zz + (kind + zz) % 2

    def send(src, dst, send_sem, recv_sem, dev):
        pltpu.make_async_remote_copy(
            src_ref=src, dst_ref=dst, send_sem=send_sem, recv_sem=recv_sem,
            device_id=dev, device_id_type=MESH,
        ).start()

    def wait(ref, sem):
        pltpu.make_async_copy(ref, ref, sem).wait()

    pending = []

    def drain():
        for ref, sem in pending:
            wait(ref, sem)
        for i in list(left):
            arrived(i)

    def arrived(i):
        local[i].wait()
        left.remove(i)

    local = [
        pltpu.make_async_copy(q_ref.at[:, pl.ds(pl.multiple_of(g * 1024, 1024), 1024)], q_v, lsem.at[0]),
        pltpu.make_async_copy(kn_ref, kn_v, lsem.at[1]),
        pltpu.make_async_copy(vn_ref, vn_v, lsem.at[2]),
        pltpu.make_async_copy(kc_ref, kc_v, lsem.at[3]),
        pltpu.make_async_copy(vc_ref, vc_v, lsem.at[4]),
        pltpu.make_async_copy(past_ref, past_v, lsem.at[5]),
        pltpu.make_async_copy(w_ref, w_v, lsem.at[6]),
        pltpu.make_async_copy(hid_ref.at[pl.ds(pl.multiple_of(v * 16, 16), 16)], hid_v, lsem.at[7]),
        pltpu.make_async_copy(hw_ref, hw_v, lsem.at[8]),
        pltpu.make_async_copy(par_ref, par_s, lsem.at[9]),
        pltpu.make_async_copy(pl_ref, par_v, lsem.at[10]),
        pltpu.make_async_copy(tl_ref, tok_v, lsem.at[11]),
        pltpu.make_async_copy(gain_ref, gain_v, lsem.at[12]),
    ]
    left = list(range(len(local)))
    for copy in local:
        copy.start()

    bar = pltpu.get_barrier_semaphore()

    def greet(d, _):
        pl.semaphore_signal(bar, inc=1, device_id=(b, (v + d) % 16), device_id_type=MESH)
        pl.semaphore_signal(bar, inc=1, device_id=((b + d) % 16, v), device_id_type=MESH)
        return 0

    def greet_pair(d, _):
        pl.semaphore_signal(
            bar, inc=1, device_id=(2 * ((z + d) % 8) + c, 2 * g + 1 - h), device_id_type=MESH
        )
        return 0

    lax.fori_loop(1, 16, greet, 0)
    lax.fori_loop(1, 8, greet_pair, 0)

    for i in range(3):
        arrived(i)
    lane_g = pl.ds(pl.multiple_of(g * 128, 128), 128)
    packed = jnp.concatenate(
        [q_v[...].astype(F32), kn_v[:, lane_g].astype(F32), vn_v[:, lane_g].astype(F32)], axis=1
    )
    upper = h.astype(F32)
    packed = packed[0:8] * (1.0 - upper) + packed[8:16] * upper
    packed = jnp.concatenate([packed[:, :640], packed[:, 640:]], axis=0).astype(BF16)
    xs[...] = packed
    xr[z] = packed

    pl.semaphore_wait(bar, 37)

    def send_query(d, _):
        zz = (z + d) % 8
        send(xs, xr.at[z], ssem.at[0], rsem.at[0], (same_kind(zz), v))
        return 0

    lax.fori_loop(1, 8, send_query, 0)
    pending.append((xr.at[0:7], ssem.at[0]))

    def cache_part(ref, target):
        rows = pl.ds(pl.multiple_of((target % 2) * 8, 8), 8)
        return ref.at[rows, :, pl.ds(pl.multiple_of((target // 2) * 128, 128), 128)]

    my_pos = pl.ds(pl.multiple_of(v * 16, 16), 16)

    def turn(ref, out, i):
        def step(d, _):
            t = (v + d) % 16
            send(cache_part(ref, t), out.at[:, my_pos, :], ssem.at[i], rsem.at[i], (b, t))
            return 0

        lax.fori_loop(1, 16, step, 0)
        pltpu.make_async_copy(cache_part(ref, v), out.at[:, my_pos, :], rsem.at[i]).start()

    turn(kc_ref, kt, 1)
    pending.append((kt.at[:, 0:240], ssem.at[1]))
    turn(vc_ref, vt, 2)
    pending.append((vt.at[:, 0:240], ssem.at[2]))

    for i in (3, 4, 9):
        arrived(i)

    def stage(zz, _):
        base = same_kind(zz) * 16
        count = jnp.int32(0)
        rows = [jnp.int32(0)] * 4
        for r in range(16):
            mine = (par_s[base + r] // 32 == z).astype(jnp.int32)
            for k in range(4):
                rows[k] = jnp.where(count * mine + mine == k + 1, r, rows[k])
            count = count + mine
        for k in range(4):
            ks[zz, k] = kc_v[rows[k]]
            vs[zz, k] = vc_v[rows[k]]
        return 0

    lax.fori_loop(0, 8, stage, 0)
    kr[z] = ks[z]
    vr[z] = vs[z]

    def bulk(src, dst, i, distances):
        for d in distances:
            zz = (z + d) % 8
            send(src.at[zz], dst.at[z], ssem.at[i], rsem.at[i], (same_kind(zz), v))

    bulk(ks, kr, 3, BULK_EARLY_K)

    lanes = iota((128, 1024), 1)
    wanted = (lanes % 128) * 8 + lanes // 128
    subs = iota((128, 1024), 0)

    def build(t, _):
        perm[pl.ds(pl.multiple_of(t * 128, 128), 128), :] = (subs + t * 128 == wanted).astype(F32).astype(BF16)
        return 0

    lax.fori_loop(0, 8, build, 0)
    k64 = iota((64, 64), 0)
    swap = (iota((64, 64), 1) == (k64 % 8) * 8 + k64 // 8).astype(F32).astype(BF16)

    for i in (5, 10, 11):
        arrived(i)
    chosen = (iota((256, 256), 0) == par_v[...]).astype(F32)
    of_parent = jnp.dot(past_v[...], chosen, precision=lax.Precision.HIGHEST, preferred_element_type=F32)
    own_token = iota((501, 256), 0) == tok_v[...] - (b * 16 + v) * 501
    acc[496:504] = jnp.zeros((8, 256), F32)
    acc[0:501] = jnp.where(own_token, of_parent, 0.0)
    picked = jnp.sum(acc[...], axis=0, keepdims=True)
    acc[496:504] = jnp.full((8, 256), -1e30, F32)

    wait(xr.at[0:7], rsem.at[0])
    got = xr[...].astype(F32)
    got = jnp.concatenate(
        [got[:, 0:8, :].reshape(64, 640), got[:, 8:16, :].reshape(64, 640)], axis=1
    ).astype(BF16)
    got = jnp.dot(swap, got, preferred_element_type=F32)
    kn_s[...] = got[:, 1024:1152]
    vn_s[...] = got[:, 1152:1280]
    qp[...] = jnp.dot(got[:, :1024].astype(BF16), perm[...], preferred_element_type=F32)
    wait(kt, rsem.at[1])
    lane256 = iota((64, 256), 1)

    def weigh(r, _):
        rows = pl.ds(pl.multiple_of(r * 8, 8), 8)
        qr = qp[rows, :]
        qf = jnp.concatenate([qr[:, j * 128:(j + 1) * 128] for j in range(8)], axis=0)
        new_key = jnp.concatenate([kn_s[rows, :]] * 8, axis=0)
        new_value = jnp.concatenate([vn_s[rows, :]] * 8, axis=0)
        s = lax.dot_general(qf.astype(BF16), kt[r], NT, preferred_element_type=F32)
        s_new = jnp.sum(qf * new_key, axis=1, keepdims=True)
        s = jnp.where(lane256 == 255, s_new, s) * HEAD_DIM ** (-0.5)
        e = jnp.exp(s - jnp.max(s, axis=1, keepdims=True))
        wf = (e / jnp.sum(e, axis=1, keepdims=True)).astype(BF16).astype(F32)
        w_s[r] = jnp.where(lane256 == 255, 0.0, wf).astype(BF16)
        o_new[r] = wf[:, 255:256] * new_value
        return 0

    lax.fori_loop(0, 8, weigh, 0, unroll=4)
    wait(vt, rsem.at[2])

    def mix(r, _):
        rows = pl.ds(pl.multiple_of(r * 8, 8), 8)
        o = jnp.dot(w_s[r], vt[r], preferred_element_type=F32) + o_new[r]
        o_s[rows, :] = jnp.concatenate([o[j * 8:(j + 1) * 8] for j in range(8)], axis=1)
        return 0

    lax.fori_loop(0, 8, mix, 0, unroll=4)
    o = lax.dot_general(o_s[...].astype(BF16), perm[...], NT, preferred_element_type=F32).astype(BF16)
    o = jnp.dot(swap, o, preferred_element_type=F32).reshape(8, 8, 1024)
    rs[...] = jnp.concatenate([o[:, :, :512], o[:, :, 512:]], axis=1).astype(BF16)
    ar[z] = rs[z]

    def send_back(d, _):
        zz = (z + d) % 8
        send(rs.at[zz], ar.at[z], ssem.at[5], rsem.at[5], (same_kind(zz), v))
        return 0

    lax.fori_loop(1, 8, send_back, 0)
    pending.append((ar.at[0:7], ssem.at[5]))
    sub16 = iota((16, 512), 0)
    beam = jnp.zeros((16, 512), jnp.int32)
    for r in range(8):
        beam = jnp.where(sub16 % 8 == r, par_s[b * 16 + h * 8 + r] // 32, beam)
    wait(ar.at[0:7], rsem.at[5])
    att = jnp.zeros((16, 512), F32)
    for p in range(8):
        att = jnp.where(beam == p, ar[p].astype(F32), att)
    for hh in range(2):
        part = att[hh * 8:hh * 8 + 8]
        a_s[hh] = jnp.concatenate([part[:, :256], part[:, 256:]], axis=0).astype(BF16)
    aa[16 * c + 2 * z + h] = a_s[h]

    slot = aa.at[16 * c + 2 * z + h]
    send(a_s.at[1 - h], slot, ssem.at[6], rsem.at[6], (b, 2 * g + 1 - h))

    def spread(d, _):
        zz = (z + d) % 8
        for hh in range(2):
            send(a_s.at[hh], slot, ssem.at[6], rsem.at[6], (2 * zz + c, 2 * g + hh))
        return 0

    lax.fori_loop(1, 8, spread, 0)
    pending.append((aa.at[0:15], ssem.at[6]))
    for i in (6, 7, 12):
        arrived(i)
    wait(aa.at[0:15], rsem.at[6])
    share = aa.at[pl.ds(16 * c, 16)]
    send(share, share, ssem.at[15], rsem.at[15], (2 * z + 1 - c, v))
    wait(aa.at[0:16], rsem.at[15])
    pending.append((aa.at[0:16], ssem.at[15]))
    rows_in = aa[...].astype(F32)
    rows_in = jnp.concatenate(
        [rows_in[:, 0:8, :].reshape(256, 256), rows_in[:, 8:16, :].reshape(256, 256)], axis=1
    ).astype(BF16)
    ps[...] = jnp.dot(rows_in, w_v[...], preferred_element_type=F32).astype(BF16).reshape(16, 16, 512)
    pr[v] = ps[(v % 2) * 8 + v // 2]

    def send_partial(d, _):
        t = (v + d) % 16
        send(ps.at[(t % 2) * 8 + t // 2], pr.at[v], ssem.at[7], rsem.at[7], (b, t))
        return 0

    lax.fori_loop(1, 16, send_partial, 0)
    pending.append((pr.at[0:15], ssem.at[7]))
    bulk(vs, vr, 4, BULK_MID_V)
    wait(pr.at[0:15], rsem.at[7])
    residual = hid_v[...].astype(F32) + jnp.sum(pr[...].astype(F32), axis=0)
    nb[c, v, 0] = (residual * gain_v[...]).astype(BF16)

    for slot in (1, 2, 3, 4, 5, 6, 7):
        zz = (z - AWAY[slot]) % 8
        send(nb.at[c, v, 0], nb.at[c, v, slot], ssem.at[8], rsem.at[8 if slot < 4 else 14], (2 * zz + c, v))
    pending.append((nb.at[0, 0, 0:7], ssem.at[8]))
    lane256 = iota((16, 256), 1)
    square = jnp.sum(residual * residual, axis=1, keepdims=True)
    square = jnp.where(lane256 == iota((16, 256), 0) + 16 * v, square, 0.0)
    square = jnp.sum(square, axis=0, keepdims=True)
    sq_s[...] = square
    sq_r[b] = square

    def send_square(d, _):
        send(sq_s, sq_r.at[b], ssem.at[9], rsem.at[9], ((b + d) % 16, v))
        return 0

    lax.fori_loop(1, 16, send_square, 0)
    pending.append((sq_r.at[0:15], ssem.at[9]))

    def along(u, axis, d):
        if axis == 0:
            return ((u // 4 + d) % 4) * 4 + u % 4
        return (u // 4) * 4 + (u % 4 + d) % 4

    def piece(u, half, part=None):
        if part is None:
            return nb.at[c, u, 4 * half:4 * half + 4]
        return nb.at[c, u, 4 * half + 2 * part:4 * half + 2 * part + 2]

    def state(ref, axis, d, sem):
        send(ref, ref, ssem.at[10], sem, (b, along(v, axis, d)))

    def sibling(ref):
        send(ref, ref, ssem.at[11], rsem.at[10], (2 * z + 1 - c, v))

    halves = ((1, 0), (0, 1))

    def first(half, order=halves):
        axis = order[half][0]
        state(piece(v, half), axis, 1, s1.at[half, 0])
        state(piece(v, half), axis, -1, s1.at[half, 1])
        state(piece(v, half), axis, 2, s2.at[half])

    def second(half, o):
        u = along(v, halves[half][0], o)
        axis = halves[half][1]
        state(piece(u, half), axis, 1, t1.at[half, o, 0])
        state(piece(u, half), axis, -1, t1.at[half, o, 1])
        if o == 2:
            state(piece(u, half), axis, 2, t2.at[half, o, 0])

    def second_forward(half, o):
        u = along(v, halves[half][0], o)
        axis = halves[half][1]
        wait(piece(u, half), t1.at[half, o, 0])
        state(piece(along(u, axis, -1), half, 0), axis, 1, t2.at[half, o, 0])
        sibling(piece(along(u, axis, -1), half))
        wait(piece(u, half), t1.at[half, o, 1])
        state(piece(along(u, axis, 1), half, 1), axis, -1, t2.at[half, o, 1])
        sibling(piece(along(u, axis, 1), half))

    for half in range(2):
        if half == 0:
            wait(nb.at[0, 0, 0:3], rsem.at[8])
        else:
            wait(nb.at[0, 0, 0:4], rsem.at[14])
        first(half)
        second(half, 0)
        sibling(piece(v, half))
    for half in range(2):
        wait(piece(v, half), s1.at[half, 0])
        second(half, 3)
        wait(piece(v, half), s1.at[half, 1])
        second(half, 1)
        sibling(piece(along(v, halves[half][0], -1), half))
        sibling(piece(along(v, halves[half][0], 1), half))
    bulk(ks, kr, 3, BULK_LATE_K)
    bulk(vs, vr, 4, BULK_LATE_V)
    for half in range(2):
        second_forward(half, 0)
    for half in range(2):
        wait(piece(v, half), s2.at[half])
        second(half, 2)
        sibling(piece(along(v, halves[half][0], 2), half))

    wait(sq_r.at[0:15], rsem.at[9])
    scale = lax.rsqrt(jnp.sum(sq_r[...], axis=0) / D + 1e-05)
    scale = jnp.where(iota((1, 256), 1) // 16 == v, scale, 0.0)
    sc_s[...] = scale
    sc_r[v] = scale

    def send_scale(d, _):
        send(sc_s, sc_r.at[v], ssem.at[12], rsem.at[11], (b, (v + d) % 16))
        return 0

    lax.fori_loop(1, 16, send_scale, 0)
    pending.append((sc_r.at[0:15], ssem.at[12]))
    for o in (3, 1):
        for half in range(2):
            second_forward(half, o)
    for o in (0, 3, 1, 2):
        for half in range(2):
            u = along(v, halves[half][0], o)
            axis = halves[half][1]
            if o == 2:
                for k in range(2):
                    wait(piece(u, half), t1.at[half, o, k])
                    sibling(piece(along(u, axis, 2 * k - 1), half))
                wait(piece(u, half), t2.at[half, o, 0])
            else:
                wait(piece(u, half, 0), t2.at[half, o, 0])
                wait(piece(u, half, 1), t2.at[half, o, 1])
            sibling(piece(along(u, axis, 2), half))

    pending.append((nb.at[0, 0:15], ssem.at[10]))
    pending.append((nb.at[0], ssem.at[11]))

    arrived(8)

    def product(core, slot):
        away = jnp.where(slot % 2 == 1, (slot + 1) // 2, (8 - slot // 2) % 8)
        cols = pl.ds(pl.multiple_of((2 * ((z + away) % 8) + core) * 512, 512), 512)
        return lax.dot_general(
            hw_v[:, cols], nb[core, :, slot].reshape(256, 512), NT, preferred_element_type=F32
        )

    def four(core, first_slot):
        return sum(product(core, first_slot + k) for k in range(1, 4)) + product(core, first_slot)

    acc[0:501] = four(c, 0)
    acc[0:501] += four(c, 4)
    wait(nb.at[0], rsem.at[10])

    acc[0:501] += four(1 - c, 0)
    acc[0:501] += four(1 - c, 4)
    wait(sc_r.at[0:15], rsem.at[11])
    logits = acc[...] * jnp.sum(sc_r[...], axis=0)
    acc[...] = logits
    largest = jnp.max(logits, axis=0, keepdims=True)
    total = jnp.sum(jnp.exp(logits - largest), axis=0, keepdims=True)

    def merged(stats):
        high = jnp.max(stats[:, 0:1], axis=0)
        total = jnp.sum(stats[:, 1:2] * jnp.exp(stats[:, 0:1] - high), axis=0)
        return jnp.concatenate([high, total, jnp.sum(stats[:, 2:4], axis=0)], axis=0)

    stats = jnp.concatenate([largest, total, picked, jnp.zeros((1, 256), F32)], axis=0)
    lv_s[...] = stats
    lv_r[v] = stats

    def send_vocab(d, _):
        send(lv_s, lv_r.at[v], ssem.at[13], rsem.at[12], (b, (v + d) % 16))
        return 0

    lax.fori_loop(1, 16, send_vocab, 0)
    pending.append((lv_r.at[0:15], ssem.at[13]))
    wait(lv_r.at[0:15], rsem.at[12])
    stats = merged(lv_r[...])
    lb_s[...] = stats
    lb_r[b] = stats

    def send_batch(d, _):
        send(lb_s, lb_r.at[b], ssem.at[14], rsem.at[13], ((b + d) % 16, v))
        return 0

    lax.fori_loop(1, 16, send_batch, 0)
    pending.append((lb_r.at[0:15], ssem.at[14]))

    wait(kr.at[0:7], rsem.at[3])
    wait(vr.at[0:7], rsem.at[4])
    last = iota((16, 1024), 0) == jnp.where(v == 15, 15, 99)
    new_keys = kn_v[...].astype(F32)
    new_values = vn_v[...].astype(F32)
    beams = [par_s[b * 16 + r] // 32 for r in range(16)]
    for r in range(16):
        at = jnp.int32(0)
        for earlier in range(r):
            at = at + (beams[earlier] == beams[r]).astype(jnp.int32)
        at = jnp.minimum(at, 3)
        nk_s[r] = jnp.where(last, new_keys[r:r + 1], kr[beams[r], at].astype(F32)).astype(BF16)
        nv_s[r] = jnp.where(last, new_values[r:r + 1], vr[beams[r], at].astype(F32)).astype(BF16)

    results = [
        pltpu.make_async_copy(nk_s, nk_ref, lsem.at[13]),
        pltpu.make_async_copy(nv_s, nv_ref, lsem.at[14]),
    ]
    for copy in results:
        copy.start()
    wait(lb_r.at[0:15], rsem.at[13])
    stats = merged(lb_r[...])
    cand_ref[...] = acc[0:501] + (stats[2:3] - (stats[0:1] + jnp.log(stats[1:2])))

    for copy in results:
        copy.wait()
    pending.append((kr.at[0:7], ssem.at[3]))
    pending.append((vr.at[0:7], ssem.at[4]))
    drain()


def deliver(nk_in, nv_in, cand_in, nk_out, nv_out, cand_out, nk_v, nv_v, cand_v, sem):
    steps = ((nk_in, nk_v, nk_out), (nv_in, nv_v, nv_out), (cand_in, cand_v, cand_out))
    loads = [pltpu.make_async_copy(src, held, sem.at[0, i]) for i, (src, held, _) in enumerate(steps)]
    stores = [pltpu.make_async_copy(held, dst, sem.at[1, i]) for i, (_, held, dst) in enumerate(steps)]
    for load in loads:
        load.start()
    for load, store in zip(loads, stores):
        load.wait()
        store.start()
    for store in stores:
        store.wait()


def body(
    queries, key_new, value_new, key_cache, value_cache, parents, tokens, hidden, out_weight, final_gain,
    head_weight, past_scores,
):
    hbm = pl.BlockSpec(memory_space=pltpu.HBM)
    vmem = pl.BlockSpec(memory_space=pltpu.VMEM)
    V = pltpu.VMEM
    scratch = [
        V((16, 1024), BF16), V((16, 1024), BF16), V((16, 1024), BF16),
        V((16, 16, 1024), BF16), V((16, 16, 1024), BF16),
        pltpu.SMEM((256,), jnp.int32), V((1, 256), jnp.int32), V((1, 256), jnp.int32),
        V((16, 512), BF16), V((512, 512), BF16), V((1, 512), F32),
        V((501, 8192), BF16), V((501, 256), F32),
        V((8, 256, 128), BF16), V((8, 256, 128), BF16),
        V((16, 640), BF16), V((8, 16, 640), BF16), V((1024, 1024), BF16),
        V((64, 1024), F32), V((64, 128), F32), V((64, 128), F32),
        V((8, 64, 256), BF16), V((8, 64, 128), F32), V((64, 1024), F32),
        V((8, 16, 512), BF16), V((8, 16, 512), BF16),
        V((2, 16, 256), BF16), V((32, 16, 256), BF16),
        V((16, 16, 512), BF16), V((16, 16, 512), BF16),
        V((8, 4, 16, 1024), BF16), V((8, 4, 16, 1024), BF16),
        V((8, 4, 16, 1024), BF16), V((8, 4, 16, 1024), BF16),
        V((2, 16, 8, 16, 512), BF16),
        V((1, 256), F32), V((16, 1, 256), F32), V((1, 256), F32), V((16, 1, 256), F32),
        V((504, 256), F32), V((16, 16, 1024), BF16), V((16, 16, 1024), BF16),
        V((4, 256), F32), V((16, 4, 256), F32), V((4, 256), F32), V((16, 4, 256), F32),
        pltpu.SemaphoreType.DMA((15,)), pltpu.SemaphoreType.DMA((16,)), pltpu.SemaphoreType.DMA((16,)),
        pltpu.SemaphoreType.DMA((2, 2)), pltpu.SemaphoreType.DMA((2,)),
        pltpu.SemaphoreType.DMA((2, 4, 2)), pltpu.SemaphoreType.DMA((2, 4, 2)),
    ]
    next_keys, next_values, scores = pl.pallas_call(
        kernel,
        out_shape=(
            jax.ShapeDtypeStruct((16, 16, 1024), BF16),
            jax.ShapeDtypeStruct((16, 16, 1024), BF16),
            jax.ShapeDtypeStruct((501, 256), F32),
        ),
        in_specs=[hbm] * 13,
        out_specs=(hbm, hbm, vmem),
        scratch_shapes=scratch,
        compiler_params=pltpu.CompilerParams(
            collective_id=0, has_side_effects=True, vmem_limit_bytes=62 * 1024 * 1024
        ),
        name="beam_step",
    )(
        queries, key_new, value_new, key_cache, value_cache, parents, parents.reshape(1, 256), tokens.reshape(1, 256),
        hidden, out_weight, final_gain.reshape(1, 512), head_weight, past_scores.T,
    )
    next_keys, next_values, scores = pl.pallas_call(
        deliver,
        out_shape=(
            jax.ShapeDtypeStruct((16, 16, 1024), BF16),
            jax.ShapeDtypeStruct((16, 16, 1024), BF16),
            jax.ShapeDtypeStruct((501, 256), F32),
        ),
        in_specs=[hbm] * 3,
        out_specs=(hbm,) * 3,
        scratch_shapes=[
            V((16, 16, 1024), BF16), V((16, 16, 1024), BF16), V((501, 256), F32),
            pltpu.SemaphoreType.DMA((2, 3)),
        ],
        compiler_params=pltpu.CompilerParams(vmem_limit_bytes=62 * 1024 * 1024),
        name="deliver",
    )(next_keys, next_values, scores)
    return next_keys, next_values, scores.T


def solution(mesh):
    in_specs = (
        P("batch", None), P("batch", None), P("batch", None),
        P("batch", "vocab", None), P("batch", "vocab", None),
        P(), P(), P(None, "batch"), P("vocab", "batch"), P("batch"),
        P(("batch", "vocab"), None), P(None, ("batch", "vocab")),
    )
    out_specs = (P("batch", "vocab", None), P("batch", "vocab", None), P(None, ("batch", "vocab")))
    return jax.shard_map(body, mesh=mesh, in_specs=in_specs, out_specs=out_specs, check_vma=False)
```

time: 119 us -> 94.4 us (0.79)
  local copies, waits for them, and re-layouts: 12.4 us -> 0 us
  Pallas kernels: 105 us -> 93.7 us
    pallas_call x1, Pallas kernels: 105 us -> 91.4 us  [body(): pl.pallas_call(kernel, out_shape=(jax.ShapeDtypeStruct((16, 16, 1024), BF...]
    unnamed x23 -> x0, local copies, waits for them, and re-layouts: 11.4 us -> none
    pallas_call x0 -> x1, Pallas kernels: none -> 2.23 us  [body(): pl.pallas_call(deliver, out_shape=(jax.ShapeDtypeStruct((16, 16, 1024), B...]
where the time goes in v2:
time: 94.4 us; the launch traced here: 94.3 us
  Pallas kernels  93.7 us (99%)
    pallas_call x1, Pallas kernels, body(): pl.pallas_call(kernel, out_shape=(jax.ShapeDtypeStruct((16, 16, 1024), BF...  91.4 us
    pallas_call x1, Pallas kernels, body(): pl.pallas_call(deliver, out_shape=(jax.ShapeDtypeStruct((16, 16, 1024), B...  2.23 us

profile of v2, /device:TPU:1, one launch (start us, length us, event | category | flops | bytes accessed | tf_op | source)
XLA Modules:
  0.0 94.3 jit_solution(14388388558934784868)
XLA Ops:
  0.6 91.4 %beam_step.1 = (bf16[16,16,1024]{2,1,0:T(8,128)(2,1)}, bf16[16,16,1024]{2,1,0:T(8,128)(2,1)}, f32[501,256]{1,0:T(8,128)}) custom-call(bf16[16,8192]{1,0:T(8,128)(2,1)} %q_ref.1, bf16[16,1024]{1,0:T(8,128)(2,1)} %kn_ref.1, bf16[16,1024]{1,0:T(8,128)(2,1)} %vn_ref.1, bf16[16,16,1024]{2,1,0:T(8,128)(2,1)} %kc_ref.1, bf16[16,16,1024]{2,1,0:T(8,128)(2,1)} %vc_ref.1, ...), custom_call_target="tpu_custom_call" | custom-call | tf_op jit(solution)/shard_map/beam_step/pallas_call | solution.py:534
  92.1 2.2 %deliver.1 = (bf16[16,16,1024]{2,1,0:T(8,128)(2,1)}, bf16[16,16,1024]{2,1,0:T(8,128)(2,1)}, f32[501,256]{1,0:T(8,128)}) custom-call(bf16[16,16,1024]{2,1,0:T(8,128)(2,1)} %get-tuple-element.9.nk_in, bf16[16,16,1024]{2,1,0:T(8,128)(2,1)} %get-tuple-element.10.nv_in, f32[501,256]{1,0:T(8,128)} %get-tuple-element.11.cand_in), custom_call_target="tpu_custom_call" | custom-call | tf_op jit(solution)/shard_map/deliver/pallas_call | solution.py:552

commit v3 on v2

--- a/solution.py
+++ b/solution.py
@@ -14,10 +14,13 @@
 BF16 = jnp.bfloat16
 NT = (((1,), (1,)), ((), ()))
 
-BULK_EARLY_K = (1, 7, 2, 6, 4)
-BULK_MID_V = (4,)
+BULK_EARLY_K = (2, 6)
+BULK_EARLY_V = (2, 6)
+BULK_BACK_K = (1, 7)
+BULK_SPREAD_V = (1, 7)
+BULK_MID_K = (4,)
 BULK_LATE_K = (3, 5)
-BULK_LATE_V = (1, 7, 2, 6, 3, 5)
+BULK_LATE_V = (4, 3, 5)
 AWAY = (0, 1, 7, 2, 6, 3, 5, 4)
 
 
@@ -63,6 +66,26 @@
     def arrived(i):
         local[i].wait()
         left.remove(i)
+
+    bar = pltpu.get_barrier_semaphore()
+
+    def greet(d, _):
+        pl.semaphore_signal(bar, inc=1, device_id=(b, (v + d) % 16), device_id_type=MESH)
+        return 0
+
+    def greet_batch(d, _):
+        pl.semaphore_signal(bar, inc=1, device_id=((b + d) % 16, v), device_id_type=MESH)
+        return 0
+
+    def greet_pair(d, _):
+        pl.semaphore_signal(
+            bar, inc=1, device_id=(2 * ((z + d) % 8) + c, 2 * g + 1 - h), device_id_type=MESH
+        )
+        return 0
+
+    lax.fori_loop(1, 16, greet, 0)
+    lax.fori_loop(1, 16, greet_batch, 0)
+    lax.fori_loop(1, 8, greet_pair, 0)
 
     local = [
         pltpu.make_async_copy(q_ref.at[:, pl.ds(pl.multiple_of(g * 1024, 1024), 1024)], q_v, lsem.at[0]),
@@ -83,22 +106,6 @@
     for copy in local:
         copy.start()
 
-    bar = pltpu.get_barrier_semaphore()
-
-    def greet(d, _):
-        pl.semaphore_signal(bar, inc=1, device_id=(b, (v + d) % 16), device_id_type=MESH)
-        pl.semaphore_signal(bar, inc=1, device_id=((b + d) % 16, v), device_id_type=MESH)
-        return 0
-
-    def greet_pair(d, _):
-        pl.semaphore_signal(
-            bar, inc=1, device_id=(2 * ((z + d) % 8) + c, 2 * g + 1 - h), device_id_type=MESH
-        )
-        return 0
-
-    lax.fori_loop(1, 16, greet, 0)
-    lax.fori_loop(1, 8, greet_pair, 0)
-
     for i in range(3):
         arrived(i)
     lane_g = pl.ds(pl.multiple_of(g * 128, 128), 128)
@@ -168,6 +175,7 @@
             send(src.at[zz], dst.at[z], ssem.at[i], rsem.at[i], (same_kind(zz), v))
 
     bulk(ks, kr, 3, BULK_EARLY_K)
+    bulk(vs, vr, 4, BULK_EARLY_V)
 
     lanes = iota((128, 1024), 1)
     wanted = (lanes % 128) * 8 + lanes // 128
@@ -239,6 +247,7 @@
         return 0
 
     lax.fori_loop(1, 8, send_back, 0)
+    bulk(ks, kr, 3, BULK_BACK_K)
     pending.append((ar.at[0:7], ssem.at[5]))
     sub16 = iota((16, 512), 0)
     beam = jnp.zeros((16, 512), jnp.int32)
@@ -263,6 +272,7 @@
         return 0
 
     lax.fori_loop(1, 8, spread, 0)
+    bulk(vs, vr, 4, BULK_SPREAD_V)
     pending.append((aa.at[0:15], ssem.at[6]))
     for i in (6, 7, 12):
         arrived(i)
@@ -285,15 +295,21 @@
 
     lax.fori_loop(1, 16, send_partial, 0)
     pending.append((pr.at[0:15], ssem.at[7]))
-    bulk(vs, vr, 4, BULK_MID_V)
+    bulk(ks, kr, 3, BULK_MID_K)
     wait(pr.at[0:15], rsem.at[7])
     residual = hid_v[...].astype(F32) + jnp.sum(pr[...].astype(F32), axis=0)
     nb[c, v, 0] = (residual * gain_v[...]).astype(BF16)
 
     for slot in (1, 2, 3, 4, 5, 6, 7):
         zz = (z - AWAY[slot]) % 8
-        send(nb.at[c, v, 0], nb.at[c, v, slot], ssem.at[8], rsem.at[8 if slot < 4 else 14], (2 * zz + c, v))
+        send(nb.at[c, v, 0], nb.at[c, v, slot], ssem.at[8], rsem.at[8 if slot < 5 else 14], (2 * zz + c, v))
     pending.append((nb.at[0, 0, 0:7], ssem.at[8]))
+
+    def send_own(d, _):
+        send(nb.at[c, v, 0], nb.at[c, v, 0], ssem.at[10], rsem.at[16], (b, (v + d) % 16))
+        return 0
+
+    lax.fori_loop(1, 16, send_own, 0)
     lane256 = iota((16, 256), 1)
     square = jnp.sum(residual * residual, axis=1, keepdims=True)
     square = jnp.where(lane256 == iota((16, 256), 0) + 16 * v, square, 0.0)
@@ -314,9 +330,12 @@
         return (u // 4) * 4 + (u % 4 + d) % 4
 
     def piece(u, half, part=None):
-        if part is None:
-            return nb.at[c, u, 4 * half:4 * half + 4]
-        return nb.at[c, u, 4 * half + 2 * part:4 * half + 2 * part + 2]
+        start, size = ((1, 4), (5, 3))[half]
+        if part == 0:
+            size = 2
+        elif part == 1:
+            start, size = start + 2, size - 2
+        return nb.at[c, u, start:start + size]
 
     def state(ref, axis, d, sem):
         send(ref, ref, ssem.at[10], sem, (b, along(v, axis, d)))
@@ -352,12 +371,16 @@
 
     for half in range(2):
         if half == 0:
-            wait(nb.at[0, 0, 0:3], rsem.at[8])
+            wait(nb.at[0, 0, 0:4], rsem.at[8])
         else:
-            wait(nb.at[0, 0, 0:4], rsem.at[14])
+            wait(nb.at[0, 0, 0:3], rsem.at[14])
         first(half)
         second(half, 0)
         sibling(piece(v, half))
+    bulk(ks, kr, 3, BULK_LATE_K)
+    bulk(vs, vr, 4, BULK_LATE_V)
+    wait(nb.at[0, 0:15, 0], rsem.at[16])
+    sibling(nb.at[c, :, 0])
     for half in range(2):
         wait(piece(v, half), s1.at[half, 0])
         second(half, 3)
@@ -365,8 +388,6 @@
         second(half, 1)
         sibling(piece(along(v, halves[half][0], -1), half))
         sibling(piece(along(v, halves[half][0], 1), half))
-    bulk(ks, kr, 3, BULK_LATE_K)
-    bulk(vs, vr, 4, BULK_LATE_V)
     for half in range(2):
         second_forward(half, 0)
     for half in range(2):
@@ -527,7 +548,7 @@
         V((1, 256), F32), V((16, 1, 256), F32), V((1, 256), F32), V((16, 1, 256), F32),
         V((504, 256), F32), V((16, 16, 1024), BF16), V((16, 16, 1024), BF16),
         V((4, 256), F32), V((16, 4, 256), F32), V((4, 256), F32), V((16, 4, 256), F32),
-        pltpu.SemaphoreType.DMA((15,)), pltpu.SemaphoreType.DMA((16,)), pltpu.SemaphoreType.DMA((16,)),
+        pltpu.SemaphoreType.DMA((15,)), pltpu.SemaphoreType.DMA((17,)), pltpu.SemaphoreType.DMA((16,)),
         pltpu.SemaphoreType.DMA((2, 2)), pltpu.SemaphoreType.DMA((2,)),
         pltpu.SemaphoreType.DMA((2, 4, 2)), pltpu.SemaphoreType.DMA((2, 4, 2)),
     ]

time: 94.4 us -> 88.2 us (0.934)
  Pallas kernels: 93.7 us -> 87.5 us
    pallas_call x1, Pallas kernels: 91.4 us -> 85.3 us  [body(): pl.pallas_call(kernel, out_shape=(jax.ShapeDtypeStruct((16, 16, 1024), BF...]
where the time goes in v3:
time: 88.2 us; the launch traced here: 88.1 us
  Pallas kernels  87.5 us (99%)
    pallas_call x1, Pallas kernels, body(): pl.pallas_call(kernel, out_shape=(jax.ShapeDtypeStruct((16, 16, 1024), BF...  85.3 us
    pallas_call x1, Pallas kernels, body(): pl.pallas_call(deliver, out_shape=(jax.ShapeDtypeStruct((16, 16, 1024), B...  2.23 us

profile of v3, /device:TPU:1, one launch (start us, length us, event | category | flops | bytes accessed | tf_op | source)
XLA Modules:
  0.0 88.1 jit_solution(12547660355050205881)
XLA Ops:
  0.6 85.3 %beam_step.1 = (bf16[16,16,1024]{2,1,0:T(8,128)(2,1)}, bf16[16,16,1024]{2,1,0:T(8,128)(2,1)}, f32[501,256]{1,0:T(8,128)}) custom-call(bf16[16,8192]{1,0:T(8,128)(2,1)} %q_ref.1, bf16[16,1024]{1,0:T(8,128)(2,1)} %kn_ref.1, bf16[16,1024]{1,0:T(8,128)(2,1)} %vn_ref.1, bf16[16,16,1024]{2,1,0:T(8,128)(2,1)} %kc_ref.1, bf16[16,16,1024]{2,1,0:T(8,128)(2,1)} %vc_ref.1, ...), custom_call_target="tpu_custom_call" | custom-call | tf_op jit(solution)/shard_map/beam_step/pallas_call | solution.py:555
  85.9 2.2 %deliver.1 = (bf16[16,16,1024]{2,1,0:T(8,128)(2,1)}, bf16[16,16,1024]{2,1,0:T(8,128)(2,1)}, f32[501,256]{1,0:T(8,128)}) custom-call(bf16[16,16,1024]{2,1,0:T(8,128)(2,1)} %get-tuple-element.9.nk_in, bf16[16,16,1024]{2,1,0:T(8,128)(2,1)} %get-tuple-element.10.nv_in, f32[501,256]{1,0:T(8,128)} %get-tuple-element.11.cand_in), custom_call_target="tpu_custom_call" | custom-call | tf_op jit(solution)/shard_map/deliver/pallas_call | solution.py:573

commit v4 on v3

--- a/solution.py
+++ b/solution.py
@@ -30,7 +30,7 @@
 
 def kernel(
     q_ref, kn_ref, vn_ref, kc_ref, vc_ref, par_ref, pl_ref, tl_ref, hid_ref, w_ref, gain_ref, hw_ref, past_ref,
-    nk_ref, nv_ref, cand_ref,
+    nk_ref, nv_ref, logit_ref, offset_ref,
     q_v, kn_v, vn_v, kc_v, vc_v, par_s, par_v, tok_v, hid_v, w_v, gain_v, hw_v, past_v,
     kt, vt, xs, xr, perm, qp, kn_s, vn_s, w_s, o_new, o_s, rs, ar, a_s, aa, ps, pr,
     ks, vs, kr, vr, nb, sq_s, sq_r, sc_s, sc_r, acc, nk_s, nv_s, lv_s, lv_r, lb_s, lb_r,
@@ -340,8 +340,8 @@
     def state(ref, axis, d, sem):
         send(ref, ref, ssem.at[10], sem, (b, along(v, axis, d)))
 
-    def sibling(ref):
-        send(ref, ref, ssem.at[11], rsem.at[10], (2 * z + 1 - c, v))
+    def sibling(ref, i=10):
+        send(ref, ref, ssem.at[11], rsem.at[i], (2 * z + 1 - c, v))
 
     halves = ((1, 0), (0, 1))
 
@@ -377,10 +377,10 @@
         first(half)
         second(half, 0)
         sibling(piece(v, half))
+    bulk(vs, vr, 4, BULK_LATE_V)
     bulk(ks, kr, 3, BULK_LATE_K)
-    bulk(vs, vr, 4, BULK_LATE_V)
     wait(nb.at[0, 0:15, 0], rsem.at[16])
-    sibling(nb.at[c, :, 0])
+    sibling(nb.at[c, :, 0], 17)
     for half in range(2):
         wait(piece(v, half), s1.at[half, 0])
         second(half, 3)
@@ -410,6 +410,18 @@
     for o in (3, 1):
         for half in range(2):
             second_forward(half, o)
+    arrived(8)
+
+    def product(core, slot):
+        away = jnp.where(slot % 2 == 1, (slot + 1) // 2, (8 - slot // 2) % 8)
+        cols = pl.ds(pl.multiple_of((2 * ((z + away) % 8) + core) * 512, 512), 512)
+        return lax.dot_general(
+            hw_v[:, cols], nb[core, :, slot].reshape(256, 512), NT, preferred_element_type=F32
+        )
+
+    acc[0:501] = product(c, 0)
+    wait(nb.at[0, :, 0], rsem.at[17])
+    acc[0:501] += product(1 - c, 0)
     for o in (0, 3, 1, 2):
         for half in range(2):
             u = along(v, halves[half][0], o)
@@ -427,27 +439,24 @@
     pending.append((nb.at[0, 0:15], ssem.at[10]))
     pending.append((nb.at[0], ssem.at[11]))
 
-    arrived(8)
-
-    def product(core, slot):
-        away = jnp.where(slot % 2 == 1, (slot + 1) // 2, (8 - slot // 2) % 8)
-        cols = pl.ds(pl.multiple_of((2 * ((z + away) % 8) + core) * 512, 512), 512)
-        return lax.dot_general(
-            hw_v[:, cols], nb[core, :, slot].reshape(256, 512), NT, preferred_element_type=F32
-        )
-
-    def four(core, first_slot):
-        return sum(product(core, first_slot + k) for k in range(1, 4)) + product(core, first_slot)
-
-    acc[0:501] = four(c, 0)
-    acc[0:501] += four(c, 4)
-    wait(nb.at[0], rsem.at[10])
-
-    acc[0:501] += four(1 - c, 0)
-    acc[0:501] += four(1 - c, 4)
+    def several(core, first_slot, count):
+        return sum(product(core, first_slot + k) for k in range(1, count)) + product(core, first_slot)
+
+    acc[0:501] += several(c, 1, 4)
+    acc[0:501] += several(c, 5, 3)
+    wait(nb.at[0, 0:14], rsem.at[10])
+
+    acc[0:501] += several(1 - c, 1, 4)
+    acc[0:501] += several(1 - c, 5, 3)
     wait(sc_r.at[0:15], rsem.at[11])
     logits = acc[...] * jnp.sum(sc_r[...], axis=0)
     acc[...] = logits
+    results = [
+        pltpu.make_async_copy(acc, logit_ref, lsem.at[15]),
+        pltpu.make_async_copy(nk_s, nk_ref, lsem.at[13]),
+        pltpu.make_async_copy(nv_s, nv_ref, lsem.at[14]),
+    ]
+    results[0].start()
     largest = jnp.max(logits, axis=0, keepdims=True)
     total = jnp.sum(jnp.exp(logits - largest), axis=0, keepdims=True)
 
@@ -492,15 +501,11 @@
         nk_s[r] = jnp.where(last, new_keys[r:r + 1], kr[beams[r], at].astype(F32)).astype(BF16)
         nv_s[r] = jnp.where(last, new_values[r:r + 1], vr[beams[r], at].astype(F32)).astype(BF16)
 
-    results = [
-        pltpu.make_async_copy(nk_s, nk_ref, lsem.at[13]),
-        pltpu.make_async_copy(nv_s, nv_ref, lsem.at[14]),
-    ]
-    for copy in results:
+    for copy in results[1:]:
         copy.start()
     wait(lb_r.at[0:15], rsem.at[13])
     stats = merged(lb_r[...])
-    cand_ref[...] = acc[0:501] + (stats[2:3] - (stats[0:1] + jnp.log(stats[1:2])))
+    offset_ref[...] = stats[2:3] - (stats[0:1] + jnp.log(stats[1:2]))
 
     for copy in results:
         copy.wait()
@@ -509,15 +514,23 @@
     drain()
 
 
-def deliver(nk_in, nv_in, cand_in, nk_out, nv_out, cand_out, nk_v, nv_v, cand_v, sem):
-    steps = ((nk_in, nk_v, nk_out), (nv_in, nv_v, nv_out), (cand_in, cand_v, cand_out))
-    loads = [pltpu.make_async_copy(src, held, sem.at[0, i]) for i, (src, held, _) in enumerate(steps)]
-    stores = [pltpu.make_async_copy(held, dst, sem.at[1, i]) for i, (_, held, dst) in enumerate(steps)]
+def deliver(nk_in, nv_in, logit_in, offset_in, nk_out, nv_out, cand_out, nk_v, nv_v, logit_v, offset_v, cand_v, sem):
+    loads = [
+        pltpu.make_async_copy(src, held, sem.at[0, i])
+        for i, (src, held) in enumerate(((logit_in, logit_v), (nk_in, nk_v), (nv_in, nv_v), (offset_in, offset_v)))
+    ]
+    stores = [
+        pltpu.make_async_copy(held, dst, sem.at[1, i])
+        for i, (held, dst) in enumerate(((cand_v, cand_out), (nk_v, nk_out), (nv_v, nv_out)))
+    ]
     for load in loads:
         load.start()
-    for load, store in zip(loads, stores):
-        load.wait()
-        store.start()
+    for i in (1, 2, 0):
+        loads[i].wait()
+        if i == 0:
+            loads[3].wait()
+            cand_v[...] = logit_v[0:501] + offset_v[...]
+        stores[i].start()
     for store in stores:
         store.wait()
 
@@ -548,19 +561,20 @@
         V((1, 256), F32), V((16, 1, 256), F32), V((1, 256), F32), V((16, 1, 256), F32),
         V((504, 256), F32), V((16, 16, 1024), BF16), V((16, 16, 1024), BF16),
         V((4, 256), F32), V((16, 4, 256), F32), V((4, 256), F32), V((16, 4, 256), F32),
-        pltpu.SemaphoreType.DMA((15,)), pltpu.SemaphoreType.DMA((17,)), pltpu.SemaphoreType.DMA((16,)),
+        pltpu.SemaphoreType.DMA((16,)), pltpu.SemaphoreType.DMA((18,)), pltpu.SemaphoreType.DMA((16,)),
         pltpu.SemaphoreType.DMA((2, 2)), pltpu.SemaphoreType.DMA((2,)),
         pltpu.SemaphoreType.DMA((2, 4, 2)), pltpu.SemaphoreType.DMA((2, 4, 2)),
     ]
-    next_keys, next_values, scores = pl.pallas_call(
+    next_keys, next_values, logits, offset = pl.pallas_call(
         kernel,
         out_shape=(
             jax.ShapeDtypeStruct((16, 16, 1024), BF16),
             jax.ShapeDtypeStruct((16, 16, 1024), BF16),
-            jax.ShapeDtypeStruct((501, 256), F32),
+            jax.ShapeDtypeStruct((504, 256), F32),
+            jax.ShapeDtypeStruct((1, 256), F32),
         ),
         in_specs=[hbm] * 13,
-        out_specs=(hbm, hbm, vmem),
+        out_specs=(hbm, hbm, hbm, vmem),
         scratch_shapes=scratch,
         compiler_params=pltpu.CompilerParams(
             collective_id=0, has_side_effects=True, vmem_limit_bytes=62 * 1024 * 1024
@@ -577,15 +591,15 @@
             jax.ShapeDtypeStruct((16, 16, 1024), BF16),
             jax.ShapeDtypeStruct((501, 256), F32),
         ),
-        in_specs=[hbm] * 3,
+        in_specs=[hbm] * 4,
         out_specs=(hbm,) * 3,
         scratch_shapes=[
-            V((16, 16, 1024), BF16), V((16, 16, 1024), BF16), V((501, 256), F32),
-            pltpu.SemaphoreType.DMA((2, 3)),
+            V((16, 16, 1024), BF16), V((16, 16, 1024), BF16), V((504, 256), F32), V((1, 256), F32),
+            V((501, 256), F32), pltpu.SemaphoreType.DMA((2, 4)),
         ],
         compiler_params=pltpu.CompilerParams(vmem_limit_bytes=62 * 1024 * 1024),
         name="deliver",
-    )(next_keys, next_values, scores)
+    )(next_keys, next_values, logits, offset)
     return next_keys, next_values, scores.T
 
 

time: 88.2 us -> 87.2 us (0.989)
  Pallas kernels: 87.5 us -> 86.5 us
    pallas_call x1, Pallas kernels: 85.3 us -> 84.1 us  [body(): pl.pallas_call(kernel, out_shape=(jax.ShapeDtypeStruct((16, 16, 1024), BF...]
where the time goes in v4:
time: 87.2 us; the launch traced here: 87.1 us
  Pallas kernels  86.5 us (99%)
    pallas_call x1, Pallas kernels, body(): pl.pallas_call(kernel, out_shape=(jax.ShapeDtypeStruct((16, 16, 1024), BF...  84.1 us
    pallas_call x1, Pallas kernels, body(): pl.pallas_call(deliver, out_shape=(jax.ShapeDtypeStruct((16, 16, 1024), B...  2.4 us

profile of v4, /device:TPU:1, one launch (start us, length us, event | category | flops | bytes accessed | tf_op | source)
XLA Modules:
  0.0 87.1 jit_solution(8045236287242300213)
XLA Ops:
  0.6 84.1 %beam_step.1 = (bf16[16,16,1024]{2,1,0:T(8,128)(2,1)}, bf16[16,16,1024]{2,1,0:T(8,128)(2,1)}, f32[504,256]{1,0:T(8,128)}, f32[1,256]{1,0:T(1,128)}) custom-call(bf16[16,8192]{1,0:T(8,128)(2,1)} %q_ref.1, bf16[16,1024]{1,0:T(8,128)(2,1)} %kn_ref.1, bf16[16,1024]{1,0:T(8,128)(2,1)} %vn_ref.1, bf16[16,16,1024]{2,1,0:T(8,128)(2,1)} %kc_ref.1, ...), custom_call_target="tpu_custom_call" | custom-call | tf_op jit(solution)/shard_map/beam_step/pallas_call | solution.py:568
  84.7 2.4 %deliver.1 = (bf16[16,16,1024]{2,1,0:T(8,128)(2,1)}, bf16[16,16,1024]{2,1,0:T(8,128)(2,1)}, f32[501,256]{1,0:T(8,128)}) custom-call(bf16[16,16,1024]{2,1,0:T(8,128)(2,1)} %get-tuple-element.10.nk_in, bf16[16,16,1024]{2,1,0:T(8,128)(2,1)} %get-tuple-element.11.nv_in, f32[504,256]{1,0:T(8,128)} %get-tuple-element.12.logit_in, f32[1,256]{1,0:T(1,128)} %get-tuple-element.13.offset_in), custom_call_target="tpu_custom_call" | custom-call | tf_op jit(solution)/shard_map/deliver/pallas_call | solution.py:587

commit v5 on v4

--- a/solution.py
+++ b/solution.py
@@ -279,21 +279,31 @@
     wait(aa.at[0:15], rsem.at[6])
     share = aa.at[pl.ds(16 * c, 16)]
     send(share, share, ssem.at[15], rsem.at[15], (2 * z + 1 - c, v))
+    def project(core):
+        rows = aa[pl.ds(16 * core, 16)].astype(F32)
+        rows = jnp.concatenate(
+            [rows[:, 0:8, :].reshape(128, 256), rows[:, 8:16, :].reshape(128, 256)], axis=1
+        ).astype(BF16)
+        part = jnp.dot(rows, w_v[...], preferred_element_type=F32).astype(BF16)
+        ps[pl.ds(8 * core, 8)] = part.reshape(8, 16, 512)
+
+        def send_partial(k, _):
+            block = (v // 2 + k) % 8
+            t = 2 * block + core
+
+            @pl.when(t != v)
+            def _():
+                send(ps.at[8 * core + block], pr.at[v], ssem.at[7], rsem.at[7], (b, t))
+
+            return 0
+
+        lax.fori_loop(0, 8, send_partial, 0)
+
+    project(c)
     wait(aa.at[0:16], rsem.at[15])
     pending.append((aa.at[0:16], ssem.at[15]))
-    rows_in = aa[...].astype(F32)
-    rows_in = jnp.concatenate(
-        [rows_in[:, 0:8, :].reshape(256, 256), rows_in[:, 8:16, :].reshape(256, 256)], axis=1
-    ).astype(BF16)
-    ps[...] = jnp.dot(rows_in, w_v[...], preferred_element_type=F32).astype(BF16).reshape(16, 16, 512)
+    project(1 - c)
     pr[v] = ps[(v % 2) * 8 + v // 2]
-
-    def send_partial(d, _):
-        t = (v + d) % 16
-        send(ps.at[(t % 2) * 8 + t // 2], pr.at[v], ssem.at[7], rsem.at[7], (b, t))
-        return 0
-
-    lax.fori_loop(1, 16, send_partial, 0)
     pending.append((pr.at[0:15], ssem.at[7]))
     bulk(ks, kr, 3, BULK_MID_K)
     wait(pr.at[0:15], rsem.at[7])

time: 87.2 us -> 86.3 us (0.990)
  Pallas kernels: 86.5 us -> 85.5 us
    pallas_call x1, Pallas kernels: 84.1 us -> 83.1 us  [body(): pl.pallas_call(kernel, out_shape=(jax.ShapeDtypeStruct((16, 16, 1024), BF...]
where the time goes in v5:
time: 86.3 us; the launch traced here: 86.2 us
  Pallas kernels  85.5 us (99%)
    pallas_call x1, Pallas kernels, body(): pl.pallas_call(kernel, out_shape=(jax.ShapeDtypeStruct((16, 16, 1024), BF...  83.1 us
    pallas_call x1, Pallas kernels, body(): pl.pallas_call(deliver, out_shape=(jax.ShapeDtypeStruct((16, 16, 1024), B...  2.4 us

profile of v5, /device:TPU:1, one launch (start us, length us, event | category | flops | bytes accessed | tf_op | source)
XLA Modules:
  0.0 86.2 jit_solution(2183513014696027607)
XLA Ops:
  0.6 83.1 %beam_step.1 = (bf16[16,16,1024]{2,1,0:T(8,128)(2,1)}, bf16[16,16,1024]{2,1,0:T(8,128)(2,1)}, f32[504,256]{1,0:T(8,128)}, f32[1,256]{1,0:T(1,128)}) custom-call(bf16[16,8192]{1,0:T(8,128)(2,1)} %q_ref.1, bf16[16,1024]{1,0:T(8,128)(2,1)} %kn_ref.1, bf16[16,1024]{1,0:T(8,128)(2,1)} %vn_ref.1, bf16[16,16,1024]{2,1,0:T(8,128)(2,1)} %kc_ref.1, ...), custom_call_target="tpu_custom_call" | custom-call | tf_op jit(solution)/shard_map/beam_step/pallas_call | solution.py:578
  83.8 2.4 %deliver.1 = (bf16[16,16,1024]{2,1,0:T(8,128)(2,1)}, bf16[16,16,1024]{2,1,0:T(8,128)(2,1)}, f32[501,256]{1,0:T(8,128)}) custom-call(bf16[16,16,1024]{2,1,0:T(8,128)(2,1)} %get-tuple-element.10.nk_in, bf16[16,16,1024]{2,1,0:T(8,128)(2,1)} %get-tuple-element.11.nv_in, f32[504,256]{1,0:T(8,128)} %get-tuple-element.12.logit_in, f32[1,256]{1,0:T(1,128)} %get-tuple-element.13.offset_in), custom_call_target="tpu_custom_call" | custom-call | tf_op jit(solution)/shard_map/deliver/pallas_call | solution.py:597
